TPU v7x, 32 devices: a whole 2x2x4 slice. The times are simulated.
32 devices in a mesh: groups: 1, gy: 8 (over z, y), gx: 4 (over x, core).
Axes of the slice: x: 2, y: 2, z: 4, core: 2. Of those that a mesh axis runs over, the one named last changes fastest.
Arguments:
- features: bfloat16 [64, 128, 128], P(('groups', 'gy'), 'gx'), may hold values from -6 to 6
- scene_codes: int32 [64, 128], P(('groups', 'gy'), 'gx'), may hold values from 0 to 255
- norm_gain: float32 [128], replicated, may hold values from 0.5 to 1.5
- in_weight: bfloat16 [128, 512], replicated, may hold values from -0.5 to 0.5
- conv_weight: float32 [3, 3, 256], replicated, may hold values from -2 to 2
- conv_bias: float32 [256], replicated, may hold values from -3 to 3
- proj_weight: bfloat16 [256, 160], replicated, may hold values from -0.375 to 0.375
- step_weight: float32 [4, 8, 256], replicated, may hold values from -2 to 2
- step_bias: float32 [4, 256], replicated, may hold values from -0.5 to 0.5
- code_table: float32 [256, 256], replicated, may hold values from -1.5 to 86.4
- decay_rates: float32 [4, 16, 256], replicated, may hold values from 0 to 0.15, as said below
- skip_gain: float32 [4, 256], replicated, may hold values from 0.5 to 1.5
- out_gain: float32 [256], replicated, may hold values from 0.5 to 1.5
- out_weight: bfloat16 [256, 128], replicated, may hold values from -0.375 to 0.375
Outputs:
- block_out: bfloat16 [64, 128, 128], P(('groups', 'gy'), 'gx')
Inputs may be any that keep to these rules, and one draw needn't show every extreme that they name: `decay_rates`: positive rates.
All inputs are finite; a program needn't handle non-finite values.
Results may differ from a plain program's by a relative error of at most 0.0075.
Values may be sent and summed in bfloat16 or wider, within the bound.
A program may use at most 128 MiB of HBM per device.

v0:
```python
import functools
import math

import jax
import jax.numpy as jnp
from jax import lax
from jax.experimental import pallas as pl
from jax.experimental.pallas import tpu as pltpu
from jax.sharding import PartitionSpec as P

MESH = pl.DeviceIdType.MESH
LANES = 128


def layer_norm(values, gain):
    mean = jnp.mean(values, axis=-1, keepdims=True)
    centered = values - mean
    spread = jnp.mean(centered * centered, axis=-1, keepdims=True)
    return centered * lax.rsqrt(spread + 1e-05) * gain


def exchange_kernel(nx, ny, xr, xc, out_r, out_c, send_r, recv_r, send_c, recv_c, own_sem):
    group = lax.axis_index("groups")
    row = lax.axis_index("gy")
    col = lax.axis_index("gx")
    barrier = pltpu.get_barrier_semaphore()
    for k in range(1, nx):
        pl.semaphore_signal(
            barrier, inc=1, device_id=(group, row, lax.rem(col + k, nx)), device_id_type=MESH
        )
    for k in range(1, ny):
        pl.semaphore_signal(
            barrier, inc=1, device_id=(group, lax.rem(row + k, ny), col), device_id_type=MESH
        )
    own_r = pltpu.make_async_copy(xr.at[col], out_r.at[col], own_sem.at[0])
    own_c = pltpu.make_async_copy(xc.at[row], out_c.at[row], own_sem.at[1])
    own_r.start()
    own_c.start()
    pl.semaphore_wait(barrier, nx + ny - 2)
    copies = []
    for k in range(1, ny):
        to = lax.rem(row + k, ny)
        copies.append(
            pltpu.make_async_remote_copy(
                src_ref=xc.at[to],
                dst_ref=out_c.at[row],
                send_sem=send_c.at[k - 1],
                recv_sem=recv_c.at[k - 1],
                device_id=(group, to, col),
                device_id_type=MESH,
            )
        )
        copies[-1].start()
    for k in range(1, nx):
        to = lax.rem(col + k, nx)
        copies.append(
            pltpu.make_async_remote_copy(
                src_ref=xr.at[to],
                dst_ref=out_r.at[col],
                send_sem=send_r.at[k - 1],
                recv_sem=recv_r.at[k - 1],
                device_id=(group, row, to),
                device_id_type=MESH,
            )
        )
        copies[-1].start()
    own_r.wait()
    own_c.wait()
    for copy in copies:
        copy.wait()


def exchange(xr, xc, call):
    nx, ny = xr.shape[0], xc.shape[0]
    return pl.pallas_call(
        functools.partial(exchange_kernel, nx, ny),
        out_shape=(
            jax.ShapeDtypeStruct(xr.shape, xr.dtype),
            jax.ShapeDtypeStruct(xc.shape, xc.dtype),
        ),
        in_specs=[pl.BlockSpec(memory_space=pltpu.VMEM)] * 2,
        out_specs=(pl.BlockSpec(memory_space=pltpu.VMEM),) * 2,
        scratch_shapes=[
            pltpu.SemaphoreType.DMA((nx - 1,)),
            pltpu.SemaphoreType.DMA((nx - 1,)),
            pltpu.SemaphoreType.DMA((ny - 1,)),
            pltpu.SemaphoreType.DMA((ny - 1,)),
            pltpu.SemaphoreType.DMA((2,)),
        ],
        compiler_params=pltpu.CompilerParams(
            collective_id=call, has_side_effects=True, vmem_limit_bytes=16 * 2**20
        ),
    )(xr, xc)


def scan_kernel(states, step_r, drive_r, coef_r, rate_r, step_c, drive_c, coef_c, rate_c, y_r, y_c):
    def run(step, drive, coef, rate, out):
        length, lines = step.shape[0], step.shape[1]

        def advance(t, state):
            size, push, mix = step[t], drive[t], coef[t]
            new = []
            parts = [None] * 4
            for n in range(states):
                decay = jnp.exp2(size * rate[n])
                now = decay * state[n] + push * mix[:, n : n + 1]
                new.append(now)
                term = now * mix[:, states + n : states + n + 1]
                parts[n % 4] = term if parts[n % 4] is None else parts[n % 4] + term
            out[t] = (parts[0] + parts[1]) + (parts[2] + parts[3])
            return tuple(new)

        start = tuple(jnp.zeros((lines, LANES), jnp.float32) for _ in range(states))
        lax.fori_loop(0, length, advance, start, unroll=2)

    run(step_r, drive_r, coef_r, rate_r, y_r)
    run(step_c, drive_c, coef_c, rate_c, y_c)


def scans(row_args, col_args, states):
    return pl.pallas_call(
        functools.partial(scan_kernel, states),
        out_shape=(
            jax.ShapeDtypeStruct(row_args[0].shape, jnp.float32),
            jax.ShapeDtypeStruct(col_args[0].shape, jnp.float32),
        ),
        in_specs=[pl.BlockSpec(memory_space=pltpu.VMEM)] * 8,
        out_specs=(pl.BlockSpec(memory_space=pltpu.VMEM),) * 2,
        compiler_params=pltpu.CompilerParams(vmem_limit_bytes=32 * 2**20),
    )(*row_args, *col_args)


def fold(values):
    _, lines, length, channels = values.shape
    halves = channels // LANES
    flipped = jnp.stack([values[0], jnp.flip(values[1], 1)])
    split = flipped.reshape(2, lines, length, halves, LANES)
    return split.transpose(2, 3, 0, 1, 4).reshape(length, halves * 2 * lines, LANES)


def strip_inputs(feats, codes, conv, weights, first):
    (norm_gain, in_weight, conv_bias, proj_weight, step_weight, step_bias, code_table, decay_rates) = weights
    lines, length = codes.shape
    inner_width = in_weight.shape[1] // 2
    states, low_rank = decay_rates.shape[1], step_weight.shape[1]
    halves = inner_width // LANES
    wide = low_rank + 2 * states
    normed = layer_norm(feats.astype(jnp.float32), norm_gain).astype(jnp.bfloat16)
    inner = jnp.dot(
        normed.reshape(-1, feats.shape[2]),
        in_weight[:, :inner_width],
        preferred_element_type=jnp.float32,
    ).astype(jnp.bfloat16)
    inner = inner.reshape(lines + 2, length, inner_width)
    padded = jnp.pad(inner, ((0, 0), (1, 1), (0, 0)))
    summed = jnp.zeros((lines, length, inner_width), jnp.float32) + conv_bias
    for a in range(3):
        for b in range(3):
            summed = (
                summed + padded[a : a + lines, b : b + length].astype(jnp.float32) * conv[a, b]
            )
    signal_low = jax.nn.silu(summed).astype(jnp.bfloat16)
    signal = signal_low.astype(jnp.float32)
    coefs = jnp.dot(
        signal_low.reshape(-1, inner_width),
        proj_weight[:, first * wide : (first + 2) * wide],
        preferred_element_type=jnp.float32,
    ).reshape(lines, length, 2, wide)
    one_hot = (codes[:, :, None] == jnp.arange(code_table.shape[0])).astype(jnp.float32)
    offsets = jnp.einsum("pqk,ke->pqe", one_hot, code_table, precision=lax.Precision.HIGHEST)
    step = jax.nn.softplus(
        jnp.einsum(
            "pqdr,dre->dpqe",
            coefs[..., :low_rank],
            step_weight[first : first + 2],
            precision=lax.Precision.HIGHEST,
        )
        + step_bias[first : first + 2, None, None, :]
        + offsets
    )
    mix = coefs[..., low_rank:].transpose(2, 0, 1, 3)
    mix = jnp.stack([mix[0], jnp.flip(mix[1], 1)]).transpose(2, 0, 1, 3)
    mix = mix.reshape(length, 1, 2 * lines, 2 * states)
    mix = jnp.broadcast_to(mix, (length, halves, 2 * lines, 2 * states))
    mix = mix.reshape(length, halves * 2 * lines, 2 * states)
    rate = (decay_rates[first : first + 2] * (-1.0 / math.log(2.0))).reshape(2, states, halves, LANES)
    rate = jnp.broadcast_to(
        rate.transpose(1, 2, 0, 3)[:, :, :, None, :], (states, halves, 2, lines, LANES)
    ).reshape(states, halves * 2 * lines, LANES)
    return (fold(step), fold(step * signal), mix, rate), signal


def unfold(y, lines, channels):
    length = y.shape[0]
    y = y.reshape(length, channels // LANES, 2, lines, LANES)
    y = y[:, :, 0] + jnp.flip(y[:, :, 1], 0)
    return y.transpose(2, 0, 1, 3).reshape(lines, length, channels)


def shifted(part, axis, up):
    count = lax.axis_size(axis)
    pairs = [(i, i + 1) if up else (i + 1, i) for i in range(count - 1)]
    return lax.ppermute(part, axis, pairs)


def on_device(
    features,
    scene_codes,
    norm_gain,
    in_weight,
    conv_weight,
    conv_bias,
    proj_weight,
    step_weight,
    step_bias,
    code_table,
    decay_rates,
    skip_gain,
    out_gain,
    out_weight,
):
    nx, ny = lax.axis_size("gx"), lax.axis_size("gy")
    rows, cols, width = features.shape
    inner_width = in_weight.shape[1] // 2
    states = decay_rates.shape[1]
    rp, cp = rows // nx, cols // ny
    codes = scene_codes.astype(jnp.bfloat16)

    def payload(block, code):
        lines, length, _ = block.shape
        size = -(-(length + 1) // 16) * 16
        code = jnp.pad(code[:, None, :], ((0, 0), (0, size - length - 1), (0, width - length)))
        return jnp.concatenate([block, code], axis=1)

    row_load = payload(features, codes)
    col_load = payload(jnp.swapaxes(features, 0, 1), codes.T)
    row_size, col_size = row_load.shape[1], col_load.shape[1]
    row_load = jnp.concatenate(
        [shifted(row_load[-1:], "gy", True), row_load, shifted(row_load[:1], "gy", False)]
    )
    col_load = jnp.concatenate(
        [shifted(col_load[-1:], "gx", True), col_load, shifted(col_load[:1], "gx", False)]
    )
    xr = jnp.stack([row_load[k * rp : k * rp + rp + 2] for k in range(nx)])
    xc = jnp.stack([col_load[k * cp : k * cp + cp + 2] for k in range(ny)])
    got_r, got_c = exchange(
        xr.reshape(nx, (rp + 2) * row_size, width), xc.reshape(ny, (cp + 2) * col_size, width), 0
    )

    def assembled(got, parts, lines, size, length):
        got = got.reshape(parts, lines + 2, size, width).transpose(1, 0, 2, 3)
        feats = got[:, :, :length].reshape(lines + 2, parts * length, width)
        code = got[1:-1, :, length, :length].reshape(lines, parts * length)
        return feats, code.astype(jnp.int32)

    weights = (
        norm_gain, in_weight, conv_bias, proj_weight, step_weight, step_bias, code_table, decay_rates,
    )
    feats_r, codes_r = assembled(got_r, nx, rp, row_size, cols)
    feats_c, codes_c = assembled(got_c, ny, cp, col_size, rows)
    row_args, signal_r = strip_inputs(feats_r, codes_r, conv_weight, weights, 0)
    col_args, signal_c = strip_inputs(feats_c, codes_c, jnp.swapaxes(conv_weight, 0, 1), weights, 2)
    y_r, y_c = scans(row_args, col_args, states)
    y_r = unfold(y_r, rp, inner_width) + (skip_gain[0] + skip_gain[1]) * signal_r
    y_c = unfold(y_c, cp, inner_width) + (skip_gain[2] + skip_gain[3]) * signal_c
    y_r = y_r.astype(jnp.bfloat16).reshape(rp, nx, cols, inner_width).transpose(1, 0, 2, 3)
    y_c = y_c.astype(jnp.bfloat16).reshape(cp, ny, rows, inner_width).transpose(1, 0, 2, 3)
    back_r, back_c = exchange(
        y_r.reshape(nx, rp * cols, inner_width), y_c.reshape(ny, cp * rows, inner_width), 1
    )
    back_r = back_r.astype(jnp.float32).reshape(rows, cols, inner_width)
    back_c = back_c.astype(jnp.float32).reshape(cols, rows, inner_width)
    total = back_r + jnp.swapaxes(back_c, 0, 1)

    source = features.astype(jnp.float32)
    normed = layer_norm(source, norm_gain).astype(jnp.bfloat16)
    gate = jnp.dot(
        normed.reshape(-1, width), in_weight[:, inner_width:], preferred_element_type=jnp.float32
    ).astype(jnp.bfloat16).reshape(rows, cols, inner_width)
    normed_out = layer_norm(total, out_gain)
    mixed = (normed_out * jax.nn.silu(gate.astype(jnp.float32))).astype(jnp.bfloat16)
    added = jnp.dot(
        mixed.reshape(-1, inner_width), out_weight, preferred_element_type=jnp.float32
    ).reshape(rows, cols, width)
    return (source + added).astype(jnp.bfloat16)


def solution(mesh):
    placed = (P(("groups", "gy"), "gx", None), P(("groups", "gy"), "gx")) + (P(),) * 12
    return jax.shard_map(
        on_device,
        mesh=mesh,
        in_specs=placed,
        out_specs=P(("groups", "gy"), "gx", None),
        check_vma=False,
    )
```

profile of v0, /device:TPU:0, one launch (start us, length us, event | category | flops | bytes accessed | tf_op | source)
XLA Modules:
  0.0 75.7 jit_solution(13566160429096526850)
XLA Ops:
  0.0 0.7 convert_bitcast_fusion
  0.8 0.9 %copy.171 = bf16[8,32,128]{2,0,1:T(8,128)(2,1)S(1)} copy(bf16[8,32,128]{2,1,0:T(8,128)(2,1)} %param.14) | data formatting | bytes 131072 | tf_op args[0]
  1.8 2.4 %collective-permute-start.2 = (bf16[1,16,128]{2,1,0:T(8,128)(2,1)S(1)}, bf16[1,16,128]{2,1,0:T(8,128)(2,1)S(1)}, u32[]{:S(2)}, u32[]{:S(2)}) collective-permute-start(bf16[1,16,128]{2,1,0:T(8,128)(2,1)S(1)} %get-tuple-element.46), channel_id=1, source_target_pairs={{0,1},{1,2},{2,3},{4,5},{5,6},{6,7},{8,9},{9,10},{10,11},{12,13},{... | collective-permute-start | bytes 12296 | tf_op jit(solution)/shard_map/ppermute | solution.py:203
  4.1 1.3 %collective-permute-start.3 = (bf16[1,16,128]{2,1,0:T(8,128)(2,1)S(1)}, bf16[1,16,128]{2,1,0:T(8,128)(2,1)S(1)}, u32[]{:S(2)}, u32[]{:S(2)}) collective-permute-start(bf16[1,16,128]{2,1,0:T(8,128)(2,1)S(1)} %get-tuple-element.45), channel_id=1, source_target_pairs={{1,0},{2,1},{3,2},{5,4},{6,5},{7,6},{9,8},{10,9},{11,10},{13,12},{... | collective-permute-start | bytes 12296 | tf_op jit(solution)/shard_map/ppermute | solution.py:203
  5.5 4.4 %collective-permute-start = (bf16[1,48,128]{2,1,0:T(8,128)(2,1)S(1)}, bf16[1,48,128]{2,1,0:T(8,128)(2,1)S(1)}, u32[]{:S(2)}, u32[]{:S(2)}) collective-permute-start(bf16[1,48,128]{2,1,0:T(8,128)(2,1)S(1)} %get-tuple-element.51), channel_id=1, source_target_pairs={{0,4},{4,8},{8,12},{12,16},{16,20},{20,24},{24,28},{1,5},{5,9},{9,... | collective-permute-start | bytes 36872 | tf_op jit(solution)/shard_map/ppermute | solution.py:203
  9.9 1.3 %collective-permute-start.1 = (bf16[1,48,128]{2,1,0:T(8,128)(2,1)S(1)}, bf16[1,48,128]{2,1,0:T(8,128)(2,1)S(1)}, u32[]{:S(2)}, u32[]{:S(2)}) collective-permute-start(bf16[1,48,128]{2,1,0:T(8,128)(2,1)S(1)} %get-tuple-element.52), channel_id=1, source_target_pairs={{4,0},{8,4},{12,8},{16,12},{20,16},{24,20},{28,24},{5,1},{9,5},{13... | collective-permute-start | bytes 36872 | tf_op jit(solution)/shard_map/ppermute | solution.py:203
  11.3 0.6 fusion.85
  12.0 0.7 copy-done.12
  13.7 0.8 %convolution_convert_fusion.2 = bf16[256,256]{1,0:T(8,128)(2,1)} fusion(bf16[256,128]{1,0:T(8,128)(2,1)S(1)} %bitcast.291, bf16[128,512]{1,0:T(8,128)(2,1)S(1)} %copy-done.4), kind=kOutput, calls=%fused_computation.8 | convolution fusion | flops 16842752 | bytes 262144 | tf_op jit(solution)/shard_map/dot_general | solution.py:277
  14.9 0.6 collective-permute-done.1
  15.5 12.6 %shard_map.136 = (bf16[4,192,128]{2,1,0:T(8,128)(2,1)S(1)}, bf16[8,96,128]{2,1,0:T(8,128)(2,1)S(1)}) custom-call(bf16[4,192,128]{2,1,0:T(8,128)(2,1)S(1)} %pad_maximum_fusion.4.xr, bf16[8,96,128]{2,1,0:T(8,128)(2,1)S(1)} %bitcast_dynamic-update-slice_fusion.xc), custom_call_target="tpu_custom_call" | custom-call | tf_op jit(solution)/shard_map/pallas_call | solution.py:75
  29.9 0.7 copy-done.21
  32.2 0.9 %broadcast_multiply_fusion = (f32[2,4,64,256]{3,2,1,0:T(8,128)S(1)}, f32[2,4,64,256]{3,2,1,0:T(8,128)S(1)}) fusion(f32[4,64,256]{2,1,0:T(8,128)S(1)} %get-tuple-element.17, f32[4,64,256]{2,1,0:T(8,128)S(1)} %fusion.27, f32[2,256]{1,0:T(2,128)S(1)} %get-tuple-element.79, f32[4,8,256]{2,1,0:T(8,128)S(1)} %copy-done.8, f32[4,64,2,40]{1,3,2,0:T(8,128)S(1)} %fusion.44), kind=kOutput, calls=%fused_computation.68 | convolution fusion | flops 13762560 | bytes 1624064 | tf_op jit(solution)/shard_map/pqdr,dre->dpqe/dot_general | solution.py:172
  35.4 0.5 copy-done.14
  37.3 0.9 %broadcast_multiply_fusion.1 = (f32[2,2,128,256]{3,2,1,0:T(8,128)S(1)}, f32[2,2,128,256]{3,2,1,0:T(8,128)S(1)}) fusion(f32[2,128,256]{2,1,0:T(8,128)S(1)} %get-tuple-element.19, f32[2,128,256]{2,1,0:T(8,128)S(1)} %fusion.29, f32[2,256]{1,0:T(2,128)S(1)} %get-tuple-element.80, f32[4,8,256]{2,1,0:T(8,128)S(1)} %copy-done.8, f32[2,128,2,40]{1,3,2,0:T(8,128)S(1)} %fusion.46), kind=kOutput, calls=%fused_computation.71 | convolution fusion | flops 13762560 | bytes 1607680 | tf_op jit(solution)/shard_map/pqdr,dre->dpqe/dot_general | solution.py:172
  38.2 0.9 %fusion.79 = (f32[1,2,128,256]{3,2,1,0:T(8,128)S(1)}, f32[2,128,256]{2,1,0:T(8,128)S(1)}, f32[2,128,256]{2,1,0:T(8,128)}, f32[1,2,128,256]{3,2,1,0:T(8,128)}) fusion(f32[2,2,128,256]{3,2,1,0:T(8,128)S(1)} %get-tuple-element.83, f32[2,2,128,256]{3,2,1,0:T(8,128)S(1)} %get-tuple-element.84), kind=kLoop, calls=%fused_computation.202 | loop fusion | bytes 2097152 | tf_op jit(solution)/shard_map/slice | solution.py:136
  39.9 0.7 copy-done.3
  40.9 0.9 %copy.117 = f32[1,2,128,2,128]{4,1,0,3,2:T(2,128)} copy(f32[1,2,128,2,128]{4,3,2,1,0:T(2,128)S(1)} %stack.101) | data formatting | bytes 524288 | tf_op jit(solution)/shard_map/stack | solution.py:136
  41.8 1.1 %stack.100 = f32[1,2,128,2,128]{4,3,2,1,0:T(2,128)S(1)} reshape(f32[1,2,128,256]{3,2,1,0:T(8,128)} %get-tuple-element.88) | data formatting | bytes 524288 | tf_op jit(solution)/shard_map/stack | solution.py:136
  43.6 0.7 copy-done.2
  44.7 20.6 %shard_map.137 = (f32[128,8,128]{2,1,0:T(8,128)S(1)}, f32[64,16,128]{2,1,0:T(8,128)S(1)}) custom-call(f32[128,8,128]{2,1,0:T(8,128)S(1)} %bitcast.254, f32[128,8,128]{2,1,0:T(8,128)S(1)} %bitcast.253, f32[128,8,32]{2,1,0:T(8,128)S(1)} %bitcast.255, f32[16,8,128]{2,1,0:T(8,128)S(1)} %bitcast.265, f32[64,16,128]{2,1,0:T(8,128)S(1)} %bitcast.252, ...), custom_call_target="tpu_custom_call" | custom-call | tf_op jit(solution)/shard_map/pallas_call | solution.py:121
  66.5 7.1 %shard_map.138 = (bf16[4,64,256]{2,1,0:T(8,128)(2,1)S(1)}, bf16[8,32,256]{2,1,0:T(8,128)(2,1)S(1)}) custom-call(bf16[4,64,256]{2,1,0:T(8,128)(2,1)S(1)} %bitcast.264, bf16[8,32,256]{2,1,0:T(8,128)(2,1)S(1)} %copy_bitcast_fusion.2.xc), custom_call_target="tpu_custom_call" | custom-call | tf_op jit(solution)/shard_map/pallas_call | solution.py:75
  74.1 0.7 copy-done.5
  74.8 0.9 %fusion.2 = bf16[8,32,128]{2,1,0:T(8,128)(2,1)} fusion(bf16[8,32,128]{2,1,0:T(8,128)(2,1)S(1)} %copy-done.1, bf16[8,32,256]{2,1,0:T(8,128)(2,1)S(1)} %bitcast.298, f32[256]{0:T(256)S(1)} %copy-done.24, f32[8,32]{1,0:T(8,128)S(1)} %add_rsqrt_fusion.3, f32[8,32]{1,0:T(8,128)S(1)} %broadcast_multiply_fusion.5, bf16[8,32,256]{2,1,0:T(8,128)(2,1)S(1)} %bitcast.258, ...), kind=kOutput, calls=%fused_computation.10 | convolution fusion | flops 17661952 | bytes 723968 | tf_op jit(solution)/shard_map/dot_general | solution.py:282
  (163 shorter events, 11.8 us)
Async XLA Ops:
  0.0 31.5 %copy-start = (f32[256,256]{1,0:T(8,128)S(1)}, f32[256,256]{1,0:T(8,128)}, u32[]{:S(2)}) copy-start(f32[256,256]{1,0:T(8,128)} %param.23) | copy-start | bytes 786436
  1.7 3.7 %copy-start.1 = (bf16[8,32,128]{2,1,0:T(8,128)(2,1)S(1)}, bf16[8,32,128]{2,1,0:T(8,128)(2,1)}, u32[]{:S(2)}) copy-start(bf16[8,32,128]{2,1,0:T(8,128)(2,1)} %param.14) | copy-start | bytes 196612
  1.8 12.9 %collective-permute-start.2 = (bf16[1,16,128]{2,1,0:T(8,128)(2,1)S(1)}, bf16[1,16,128]{2,1,0:T(8,128)(2,1)S(1)}, u32[]{:S(2)}, u32[]{:S(2)}) collective-permute-start(bf16[1,16,128]{2,1,0:T(8,128)(2,1)S(1)} %get-tuple-element.46), channel_id=1, source_target_pairs={{0,1},{1,2},{2,3},{4,5},{5,6},{6,7},{8,9},{9,10},{10,11},{12,13},{... | collective-permute-start | bytes 12296 | tf_op jit(solution)/shard_map/ppermute | solution.py:203
  4.1 10.6 %collective-permute-start.3 = (bf16[1,16,128]{2,1,0:T(8,128)(2,1)S(1)}, bf16[1,16,128]{2,1,0:T(8,128)(2,1)S(1)}, u32[]{:S(2)}, u32[]{:S(2)}) collective-permute-start(bf16[1,16,128]{2,1,0:T(8,128)(2,1)S(1)} %get-tuple-element.45), channel_id=1, source_target_pairs={{1,0},{2,1},{3,2},{5,4},{6,5},{7,6},{9,8},{10,9},{11,10},{13,12},{... | collective-permute-start | bytes 12296 | tf_op jit(solution)/shard_map/ppermute | solution.py:203
  5.5 5.8 %copy-start.9 = (f32[3,3,256]{2,1,0:T(4,128)S(1)}, f32[3,3,256]{2,1,0:T(4,128)}, u32[]{:S(2)}) copy-start(f32[3,3,256]{2,1,0:T(4,128)} %param.18) | copy-start | bytes 27652
  5.5 6.5 %copy-start.6 = (bf16[256,160]{0,1:T(8,128)(2,1)S(1)}, bf16[256,160]{0,1:T(8,128)(2,1)}, u32[]{:S(2)}) copy-start(bf16[256,160]{0,1:T(8,128)(2,1)} %param.20) | copy-start | bytes 245764
  5.5 9.4 %collective-permute-start = (bf16[1,48,128]{2,1,0:T(8,128)(2,1)S(1)}, bf16[1,48,128]{2,1,0:T(8,128)(2,1)S(1)}, u32[]{:S(2)}, u32[]{:S(2)}) collective-permute-start(bf16[1,48,128]{2,1,0:T(8,128)(2,1)S(1)} %get-tuple-element.51), channel_id=1, source_target_pairs={{0,4},{4,8},{8,12},{12,16},{16,20},{20,24},{24,28},{1,5},{5,9},{9,... | collective-permute-start | bytes 36872 | tf_op jit(solution)/shard_map/ppermute | solution.py:203
  9.9 5.6 %collective-permute-start.1 = (bf16[1,48,128]{2,1,0:T(8,128)(2,1)S(1)}, bf16[1,48,128]{2,1,0:T(8,128)(2,1)S(1)}, u32[]{:S(2)}, u32[]{:S(2)}) collective-permute-start(bf16[1,48,128]{2,1,0:T(8,128)(2,1)S(1)} %get-tuple-element.52), channel_id=1, source_target_pairs={{4,0},{8,4},{12,8},{16,12},{20,16},{24,20},{28,24},{5,1},{9,5},{13... | collective-permute-start | bytes 36872 | tf_op jit(solution)/shard_map/ppermute | solution.py:203
  12.0 0.7 copy-start.12
  12.0 0.8 %copy-start.7 = (f32[4,16,256]{2,1,0:T(8,128)S(1)}, f32[4,16,256]{2,1,0:T(8,128)}, u32[]{:S(2)}) copy-start(f32[4,16,256]{2,1,0:T(8,128)} %param.24) | copy-start | bytes 196612
  12.8 0.9 %copy-start.4 = (bf16[128,512]{1,0:T(8,128)(2,1)S(1)}, bf16[128,512]{1,0:T(8,128)(2,1)}, u32[]{:S(2)}) copy-start(bf16[128,512]{1,0:T(8,128)(2,1)} %param.17) | copy-start | bytes 393220
  13.7 0.8 %copy-start.11 = (f32[4,256]{1,0:T(4,128)S(1)}, f32[4,256]{1,0:T(4,128)}, u32[]{:S(2)}) copy-start(f32[4,256]{1,0:T(4,128)} %param.25) | copy-start | bytes 12292
  29.9 0.7 copy-start.21
  31.5 0.8 %copy-start.8 = (f32[4,8,256]{2,1,0:T(8,128)S(1)}, f32[4,8,256]{2,1,0:T(8,128)}, u32[]{:S(2)}) copy-start(f32[4,8,256]{2,1,0:T(8,128)} %param.21) | copy-start | bytes 98308
  35.3 0.7 copy-start.16
  35.3 0.7 copy-start.17
  35.4 0.7 copy-start.19
  35.4 0.7 copy-start.22
  35.4 0.7 copy-start.13
  39.7 1.0 %copy-start.3 = (f32[2,128,256]{2,1,0:T(8,128)S(1)}, f32[2,128,256]{2,1,0:T(8,128)}, u32[]{:S(2)}) copy-start(f32[2,128,256]{2,1,0:T(8,128)} %get-tuple-element.87) | copy-start | bytes 786436
  43.4 1.0 %copy-start.2 = (f32[1,2,128,2,128]{4,1,0,3,2:T(2,128)S(1)}, f32[1,2,128,2,128]{4,1,0,3,2:T(2,128)}, u32[]{:S(2)}) copy-start(f32[1,2,128,2,128]{4,1,0,3,2:T(2,128)} %copy.117) | copy-start | bytes 786436
  73.8 0.9 %copy-start.5 = (bf16[256,256]{1,0:T(8,128)(2,1)S(1)}, bf16[256,256]{1,0:T(8,128)(2,1)}, u32[]{:S(2)}) copy-start(bf16[256,256]{1,0:T(8,128)(2,1)} %convolution_convert_fusion.2) | copy-start | bytes 393220
  73.9 0.9 %copy-start.23 = (bf16[256,128]{1,0:T(8,128)(2,1)S(1)}, bf16[256,128]{1,0:T(8,128)(2,1)}, u32[]{:S(2)}) copy-start(bf16[256,128]{1,0:T(8,128)(2,1)} %param.27) | copy-start | bytes 196612
  74.1 0.7 copy-start.24
  (5 other events, 3.3 us)
where the time goes:
time: 76.3 us; the launch traced here: 75.7 us
  Pallas kernels  40.3 us (53%)
  local copies, waits for them, and re-layouts  14.9 us (20%)
  starting transfers between devices  9.33 us (12%)
  matrix products  5.02 us (7%)
  other arithmetic  4.58 us (6%)
  between operations  1.01 us (1%)
    pallas_call x1, Pallas kernels, scans(): pl.pallas_call(functools.partial(scan_kernel, states), out_shape=(jax.Sha...  20.6 us
    pallas_call x2, Pallas kernels, exchange(): pl.pallas_call(functools.partial(exchange_kernel, nx, ny), out_shape=(jax...  19.7 us
    ppermute x4, starting transfers between devices, shifted(): return lax.ppermute(part, axis, pairs)  9.33 us
    unnamed x62, local copies, waits for them, and re-layouts  6.39 us
    another operation x16, local copies, waits for them, and re-layouts, fold(): flipped = jnp.stack([values[0], jnp.flip(values[1], 1)])  4.24 us
    dot_general x2, matrix products, strip_inputs(): jnp.einsum('pqdr,dre->dpqe', coefs[..., :low_rank], step_weight[first:fir...  1.84 us
  transfers between devices with their start and end apart: 4, of which 1 were waited for; matrix products, arithmetic and copies ran while one was open for 3% of the time, Pallas kernels for 0%

commit v1 on v0

--- a/solution.py
+++ b/solution.py
@@ -19,25 +19,81 @@
     return centered * lax.rsqrt(spread + 1e-05) * gain
 
 
-def exchange_kernel(nx, ny, xr, xc, out_r, out_c, send_r, recv_r, send_c, recv_c, own_sem):
+def exchange_kernel(nx, ny, halo, *refs):
+    refs = list(refs)
+    take = lambda count: [refs.pop(0) for _ in range(count)]
+    xr, xc = take(2)
+    edge_r, edge_c = take(2) if halo else (None, None)
+    out_r, out_c = take(2)
+    halo_r, halo_c = take(2) if halo else (None, None)
+    send_r, recv_r, send_c, recv_c, own_sem = take(5)
+    edge_sem, halo_r_sem, halo_c_sem = take(3) if halo else (None,) * 3
     group = lax.axis_index("groups")
     row = lax.axis_index("gy")
     col = lax.axis_index("gx")
     barrier = pltpu.get_barrier_semaphore()
+    inside_up, inside_down = row > 0, row < ny - 1
+    inside_left, inside_right = col > 0, col < nx - 1
+
+    def greet(to_row, to_col):
+        pl.semaphore_signal(barrier, inc=1, device_id=(group, to_row, to_col), device_id_type=MESH)
+
     for k in range(1, nx):
-        pl.semaphore_signal(
-            barrier, inc=1, device_id=(group, row, lax.rem(col + k, nx)), device_id_type=MESH
+        greet(row, lax.rem(col + k, nx))
+    for k in range(1, ny):
+        greet(lax.rem(row + k, ny), col)
+    if halo:
+        receives = (
+            (inside_up & (col == 0), [(lax.rem(row + ny - 1, ny), s) for s in range(nx)]),
+            (inside_down & (col == nx - 1), [(lax.rem(row + 1, ny), s) for s in range(nx)]),
+            (inside_left & (row == 0), [(s, lax.rem(col + nx - 1, nx)) for s in range(ny)]),
+            (inside_right & (row == ny - 1), [(s, lax.rem(col + 1, nx)) for s in range(ny)]),
         )
-    for k in range(1, ny):
-        pl.semaphore_signal(
-            barrier, inc=1, device_id=(group, lax.rem(row + k, ny), col), device_id_type=MESH
-        )
+        for here, sources in receives:
+
+            @pl.when(here)
+            def _(sources=sources):
+                for source in sources:
+                    greet(*source)
+
     own_r = pltpu.make_async_copy(xr.at[col], out_r.at[col], own_sem.at[0])
     own_c = pltpu.make_async_copy(xc.at[row], out_c.at[row], own_sem.at[1])
     own_r.start()
     own_c.start()
-    pl.semaphore_wait(barrier, nx + ny - 2)
+    peers = nx + ny - 2
+    if halo:
+        peers += lax.div(row + ny - 1, ny) + 1 - lax.div(row + 1, ny)
+        peers += lax.div(col + nx - 1, nx) + 1 - lax.div(col + 1, nx)
+    pl.semaphore_wait(barrier, peers)
     copies = []
+    if halo:
+        def edge(which, slot):
+            down = which % 2 == 0
+            if which < 2:
+                return pltpu.make_async_remote_copy(
+                    src_ref=edge_r.at[1 if down else 0],
+                    dst_ref=halo_r.at[which * nx + slot],
+                    send_sem=edge_sem.at[which],
+                    recv_sem=halo_r_sem.at[which * nx + slot],
+                    device_id=(group, lax.rem(row + (1 if down else ny - 1), ny), 0 if down else nx - 1),
+                    device_id_type=MESH,
+                )
+            return pltpu.make_async_remote_copy(
+                src_ref=edge_c.at[1 if down else 0],
+                dst_ref=halo_c.at[(which - 2) * ny + slot],
+                send_sem=edge_sem.at[which],
+                recv_sem=halo_c_sem.at[(which - 2) * ny + slot],
+                device_id=(group, 0 if down else ny - 1, lax.rem(col + (1 if down else nx - 1), nx)),
+                device_id_type=MESH,
+            )
+
+        sends = (inside_down, inside_up, inside_right, inside_left)
+        for which in range(4):
+
+            @pl.when(sends[which])
+            def _(which=which):
+                edge(which, col if which < 2 else row).start()
+
     for k in range(1, ny):
         to = lax.rem(row + k, ny)
         copies.append(
@@ -68,82 +124,130 @@
     own_c.wait()
     for copy in copies:
         copy.wait()
-
-
-def exchange(xr, xc, call):
+    if halo:
+        for which in range(4):
+
+            @pl.when(sends[which])
+            def _(which=which):
+                edge(which, col if which < 2 else row).wait_send()
+
+            @pl.when(receives[which][0])
+            def _(which=which):
+                for slot in range(nx if which < 2 else ny):
+                    edge(which, slot).wait_recv()
+
+
+def exchange(xr, xc, call, edges=None):
     nx, ny = xr.shape[0], xc.shape[0]
+    shapes = [xr.shape, xc.shape]
+    sems = [(nx - 1,), (nx - 1,), (ny - 1,), (ny - 1,), (2,)]
+    args = [xr, xc]
+    if edges is not None:
+        args += list(edges)
+        shapes += [(2 * nx,) + edges[0].shape[1:], (2 * ny,) + edges[1].shape[1:]]
+        sems += [(4,), (2 * nx,), (2 * ny,)]
     return pl.pallas_call(
-        functools.partial(exchange_kernel, nx, ny),
-        out_shape=(
-            jax.ShapeDtypeStruct(xr.shape, xr.dtype),
-            jax.ShapeDtypeStruct(xc.shape, xc.dtype),
-        ),
-        in_specs=[pl.BlockSpec(memory_space=pltpu.VMEM)] * 2,
-        out_specs=(pl.BlockSpec(memory_space=pltpu.VMEM),) * 2,
-        scratch_shapes=[
-            pltpu.SemaphoreType.DMA((nx - 1,)),
-            pltpu.SemaphoreType.DMA((nx - 1,)),
-            pltpu.SemaphoreType.DMA((ny - 1,)),
-            pltpu.SemaphoreType.DMA((ny - 1,)),
-            pltpu.SemaphoreType.DMA((2,)),
-        ],
+        functools.partial(exchange_kernel, nx, ny, edges is not None),
+        out_shape=tuple(jax.ShapeDtypeStruct(shape, xr.dtype) for shape in shapes),
+        in_specs=[pl.BlockSpec(memory_space=pltpu.VMEM)] * len(args),
+        out_specs=(pl.BlockSpec(memory_space=pltpu.VMEM),) * len(shapes),
+        scratch_shapes=[pltpu.SemaphoreType.DMA(shape) for shape in sems],
         compiler_params=pltpu.CompilerParams(
             collective_id=call, has_side_effects=True, vmem_limit_bytes=16 * 2**20
         ),
-    )(xr, xc)
-
-
-def scan_kernel(states, step_r, drive_r, coef_r, rate_r, step_c, drive_c, coef_c, rate_c, y_r, y_c):
+    )(*args)
+
+
+def scan_kernel(
+    states, chunk, step_r, drive_r, coef_r, rate_r, step_c, drive_c, coef_c, rate_c, y_r, y_c, pick, wide, state_ref
+):
+    place = lax.broadcasted_iota(jnp.int32, pick.shape, 0)
+    lane = lax.broadcasted_iota(jnp.int32, pick.shape, 1)
+    pick[...] = jnp.where(lax.rem(place, 2 * states) == lane // LANES, 1.0, 0.0).astype(jnp.bfloat16)
+
     def run(step, drive, coef, rate, out):
-        length, lines = step.shape[0], step.shape[1]
-
-        def advance(t, state):
-            size, push, mix = step[t], drive[t], coef[t]
-            new = []
-            parts = [None] * 4
+        length, lines, lanes = step.shape
+        copies = lanes // LANES
+        state_ref[...] = jnp.zeros_like(state_ref)
+
+        @pl.loop(0, length // chunk)
+        def _(block):
+            rows = chunk * lines
+            values = coef[pl.ds(pl.multiple_of(block * rows, rows), rows), :]
+            high = values.astype(jnp.bfloat16)
+            rest = values - high.astype(jnp.float32)
+            middle = rest.astype(jnp.bfloat16)
+            low = (rest - middle.astype(jnp.float32)).astype(jnp.bfloat16)
+            parts = jnp.concatenate([high, middle, low], axis=1)
+            wide[...] = jnp.dot(parts, pick[...], preferred_element_type=jnp.float32)
+
+            def advance(k, state):
+                t = block * chunk + k
+                at = pl.ds(pl.multiple_of(k * lines, lines), lines)
+                size, push = step[t], drive[t]
+                new, sums = [], [None, None]
+                for n in range(states):
+                    into = wide[at, n * LANES : (n + 1) * LANES]
+                    outof = wide[at, (states + n) * LANES : (states + n + 1) * LANES]
+                    if copies > 1:
+                        into = jnp.concatenate([into] * copies, axis=1)
+                        outof = jnp.concatenate([outof] * copies, axis=1)
+                    now = jnp.exp2(size * rate[n]) * state[n] + push * into
+                    new.append(now)
+                    term = now * outof
+                    sums[n % 2] = term if sums[n % 2] is None else sums[n % 2] + term
+                out[t] = sums[0] + sums[1]
+                return tuple(new)
+
+            start = tuple(state_ref[n, :, :lanes] for n in range(states))
+            end = lax.fori_loop(0, chunk, advance, start, unroll=4)
             for n in range(states):
-                decay = jnp.exp2(size * rate[n])
-                now = decay * state[n] + push * mix[:, n : n + 1]
-                new.append(now)
-                term = now * mix[:, states + n : states + n + 1]
-                parts[n % 4] = term if parts[n % 4] is None else parts[n % 4] + term
-            out[t] = (parts[0] + parts[1]) + (parts[2] + parts[3])
-            return tuple(new)
-
-        start = tuple(jnp.zeros((lines, LANES), jnp.float32) for _ in range(states))
-        lax.fori_loop(0, length, advance, start, unroll=2)
+                state_ref[n, :, :lanes] = end[n]
 
     run(step_r, drive_r, coef_r, rate_r, y_r)
     run(step_c, drive_c, coef_c, rate_c, y_c)
 
 
 def scans(row_args, col_args, states):
+    lines = row_args[0].shape[1]
+    chunk = math.gcd(16, math.gcd(row_args[0].shape[0], col_args[0].shape[0]))
     return pl.pallas_call(
-        functools.partial(scan_kernel, states),
+        functools.partial(scan_kernel, states, chunk),
         out_shape=(
             jax.ShapeDtypeStruct(row_args[0].shape, jnp.float32),
             jax.ShapeDtypeStruct(col_args[0].shape, jnp.float32),
         ),
         in_specs=[pl.BlockSpec(memory_space=pltpu.VMEM)] * 8,
         out_specs=(pl.BlockSpec(memory_space=pltpu.VMEM),) * 2,
+        scratch_shapes=[
+            pltpu.VMEM((6 * states, 2 * states * LANES), jnp.bfloat16),
+            pltpu.VMEM((chunk * lines, 2 * states * LANES), jnp.float32),
+            pltpu.VMEM((states, lines, max(row_args[0].shape[2], col_args[0].shape[2])), jnp.float32),
+        ],
         compiler_params=pltpu.CompilerParams(vmem_limit_bytes=32 * 2**20),
     )(*row_args, *col_args)
 
 
-def fold(values):
+def to_tile(values, axis):
+    pads = [(0, 0)] * values.ndim
+    pads[axis] = (0, -values.shape[axis] % 8)
+    return jnp.pad(values, pads)
+
+
+def fold(values, lanes):
     _, lines, length, channels = values.shape
-    halves = channels // LANES
+    parts = channels // lanes
     flipped = jnp.stack([values[0], jnp.flip(values[1], 1)])
-    split = flipped.reshape(2, lines, length, halves, LANES)
-    return split.transpose(2, 3, 0, 1, 4).reshape(length, halves * 2 * lines, LANES)
-
-
-def strip_inputs(feats, codes, conv, weights, first):
+    split = flipped.reshape(2, lines, length, parts, lanes)
+    return to_tile(split.transpose(2, 3, 0, 1, 4).reshape(length, parts * 2 * lines, lanes), 1)
+
+
+def strip_inputs(feats, codes, conv, weights, first, lanes):
     (norm_gain, in_weight, conv_bias, proj_weight, step_weight, step_bias, code_table, decay_rates) = weights
     lines, length = codes.shape
     inner_width = in_weight.shape[1] // 2
     states, low_rank = decay_rates.shape[1], step_weight.shape[1]
-    halves = inner_width // LANES
+    halves = inner_width // lanes
     wide = low_rank + 2 * states
     normed = layer_norm(feats.astype(jnp.float32), norm_gain).astype(jnp.bfloat16)
     inner = jnp.dot(
@@ -182,25 +286,20 @@
     mix = jnp.stack([mix[0], jnp.flip(mix[1], 1)]).transpose(2, 0, 1, 3)
     mix = mix.reshape(length, 1, 2 * lines, 2 * states)
     mix = jnp.broadcast_to(mix, (length, halves, 2 * lines, 2 * states))
-    mix = mix.reshape(length, halves * 2 * lines, 2 * states)
-    rate = (decay_rates[first : first + 2] * (-1.0 / math.log(2.0))).reshape(2, states, halves, LANES)
+    mix = to_tile(mix.reshape(length, halves * 2 * lines, 2 * states), 1).reshape(-1, 2 * states)
+    rate = (decay_rates[first : first + 2] * (-1.0 / math.log(2.0))).reshape(2, states, halves, lanes)
     rate = jnp.broadcast_to(
-        rate.transpose(1, 2, 0, 3)[:, :, :, None, :], (states, halves, 2, lines, LANES)
-    ).reshape(states, halves * 2 * lines, LANES)
-    return (fold(step), fold(step * signal), mix, rate), signal
+        rate.transpose(1, 2, 0, 3)[:, :, :, None, :], (states, halves, 2, lines, lanes)
+    ).reshape(states, halves * 2 * lines, lanes)
+    return (fold(step, lanes), fold(step * signal, lanes), mix, to_tile(rate, 1)), signal
 
 
 def unfold(y, lines, channels):
-    length = y.shape[0]
-    y = y.reshape(length, channels // LANES, 2, lines, LANES)
+    length, _, lanes = y.shape
+    parts = channels // lanes
+    y = y[:, : parts * 2 * lines].reshape(length, parts, 2, lines, lanes)
     y = y[:, :, 0] + jnp.flip(y[:, :, 1], 0)
     return y.transpose(2, 0, 1, 3).reshape(lines, length, channels)
-
-
-def shifted(part, axis, up):
-    count = lax.axis_size(axis)
-    pairs = [(i, i + 1) if up else (i + 1, i) for i in range(count - 1)]
-    return lax.ppermute(part, axis, pairs)
 
 
 def on_device(
@@ -235,31 +334,46 @@
     row_load = payload(features, codes)
     col_load = payload(jnp.swapaxes(features, 0, 1), codes.T)
     row_size, col_size = row_load.shape[1], col_load.shape[1]
-    row_load = jnp.concatenate(
-        [shifted(row_load[-1:], "gy", True), row_load, shifted(row_load[:1], "gy", False)]
-    )
-    col_load = jnp.concatenate(
-        [shifted(col_load[-1:], "gx", True), col_load, shifted(col_load[:1], "gx", False)]
-    )
+    edges = tuple(jnp.stack([load[0], load[-1]]) for load in (row_load, col_load))
+    row_load, col_load = (jnp.pad(load, ((1, 1), (0, 0), (0, 0))) for load in (row_load, col_load))
     xr = jnp.stack([row_load[k * rp : k * rp + rp + 2] for k in range(nx)])
     xc = jnp.stack([col_load[k * cp : k * cp + cp + 2] for k in range(ny)])
-    got_r, got_c = exchange(
-        xr.reshape(nx, (rp + 2) * row_size, width), xc.reshape(ny, (cp + 2) * col_size, width), 0
-    )
-
-    def assembled(got, parts, lines, size, length):
-        got = got.reshape(parts, lines + 2, size, width).transpose(1, 0, 2, 3)
-        feats = got[:, :, :length].reshape(lines + 2, parts * length, width)
-        code = got[1:-1, :, length, :length].reshape(lines, parts * length)
-        return feats, code.astype(jnp.int32)
+    got_r, got_c, halo_r, halo_c = exchange(
+        xr.reshape(nx, (rp + 2) * row_size, width),
+        xc.reshape(ny, (cp + 2) * col_size, width),
+        0,
+        edges,
+    )
+    place_x, place_y = lax.axis_index("gx"), lax.axis_index("gy")
+
+    def assembled(got, halo, parts, lines, size, length, inner, outer, inner_count, outer_count):
+        got = got.reshape(parts, lines + 2, size, width)
+        code = got[:, 1:-1, length, :length].transpose(1, 0, 2).reshape(lines, parts * length)
+        feats = got[:, :, :length].transpose(1, 0, 2, 3)
+        none = jnp.zeros_like(feats[0])
+        halo = halo.reshape(2, parts, size, width)
+        before = jnp.where(outer > 0, halo[0, :, :length], none)
+        after = jnp.where(outer < outer_count - 1, halo[1, :, :length], none)
+        feats = jnp.concatenate(
+            [
+                jnp.where(inner == 0, before, feats[0])[None],
+                feats[1:-1],
+                jnp.where(inner == inner_count - 1, after, feats[-1])[None],
+            ]
+        )
+        return feats.reshape(lines + 2, parts * length, width), code.astype(jnp.int32)
 
     weights = (
         norm_gain, in_weight, conv_bias, proj_weight, step_weight, step_bias, code_table, decay_rates,
     )
-    feats_r, codes_r = assembled(got_r, nx, rp, row_size, cols)
-    feats_c, codes_c = assembled(got_c, ny, cp, col_size, rows)
-    row_args, signal_r = strip_inputs(feats_r, codes_r, conv_weight, weights, 0)
-    col_args, signal_c = strip_inputs(feats_c, codes_c, jnp.swapaxes(conv_weight, 0, 1), weights, 2)
+    feats_r, codes_r = assembled(
+        got_r, halo_r, nx, rp, row_size, cols, place_x, place_y, nx, ny
+    )
+    feats_c, codes_c = assembled(
+        got_c, halo_c, ny, cp, col_size, rows, place_y, place_x, ny, nx
+    )
+    row_args, signal_r = strip_inputs(feats_r, codes_r, conv_weight, weights, 0, LANES)
+    col_args, signal_c = strip_inputs(feats_c, codes_c, jnp.swapaxes(conv_weight, 0, 1), weights, 2, inner_width)
     y_r, y_c = scans(row_args, col_args, states)
     y_r = unfold(y_r, rp, inner_width) + (skip_gain[0] + skip_gain[1]) * signal_r
     y_c = unfold(y_c, cp, inner_width) + (skip_gain[2] + skip_gain[3]) * signal_c

time: 76.3 us -> 62.3 us (0.82)
  Pallas kernels: 40.3 us -> 29.8 us
  starting transfers between devices: 9.33 us -> 0 us
  local copies, waits for them, and re-layouts: 14.9 us -> 21.7 us
    pallas_call x3, Pallas kernels: 40.3 us -> 29.8 us  [the longest x2 19.5 us: exchange(): pl.pallas_call(functools.partial(exchange_kernel, nx, ny, edges is not No...]
    ppermute x4 -> x0, starting transfers between devices: 9.33 us -> none  [shifted(): return lax.ppermute(part, axis, pairs)]
    unnamed x62 -> x50, local copies, waits for them, and re-layouts: 6.39 us -> 12 us
    broadcast_in_dim x2 -> x4, local copies, waits for them, and re-layouts: 0.05 us -> 1.67 us  [strip_inputs(): jnp.broadcast_to(rate.transpose(1, 2, 0, 3)[:, :, :, None, :], (states, h...]
    another operation x16 -> x8, local copies, waits for them, and re-layouts: 4.24 us -> 3.95 us  [fold(): flipped = jnp.stack([values[0], jnp.flip(values[1], 1)])]
  transfers between devices with their start and end apart: 4 -> 0, of which waited for: 1 -> 0; matrix products, arithmetic and copies ran while one was open for 3% -> 0% of each run, Pallas kernels for 0% -> 0%
where the time goes in v1:
time: 62.3 us; the launch traced here: 61.5 us
  Pallas kernels  29.8 us (48%)
  local copies, waits for them, and re-layouts  21.7 us (35%)
  other arithmetic  4.96 us (8%)
  matrix products  4.31 us (7%)
  between operations  0.83 us (1%)
    pallas_call x2, Pallas kernels, exchange(): pl.pallas_call(functools.partial(exchange_kernel, nx, ny, edges is not No...  19.5 us
    unnamed x50, local copies, waits for them, and re-layouts  12 us
    pallas_call x1, Pallas kernels, scans(): pl.pallas_call(functools.partial(scan_kernel, states, chunk), out_shape=(...  10.3 us
    another operation x8, local copies, waits for them, and re-layouts, fold(): flipped = jnp.stack([values[0], jnp.flip(values[1], 1)])  3.95 us
    dot_general x2, matrix products, strip_inputs(): jnp.einsum('pqdr,dre->dpqe', coefs[..., :low_rank], step_weight[first:fir...  1.83 us
    broadcast_in_dim x4, local copies, waits for them, and re-layouts, strip_inputs(): jnp.broadcast_to(rate.transpose(1, 2, 0, 3)[:, :, :, None, :], (states, h...  1.67 us
    convert_element_type x2, other arithmetic, strip_inputs(): signal = signal_low.astype(jnp.float32)  1.33 us

profile of v1, /device:TPU:0, one launch (start us, length us, event | category | flops | bytes accessed | tf_op | source)
XLA Modules:
  0.0 61.5 jit_solution(8785905127276141193)
XLA Ops:
  0.0 0.7 %convert_bitcast_fusion.2 = (bf16[32,1,8]{0,2,1:T(8,128)(2,1)S(1)}, bf16[8,1,32]{2,0,1:T(8,128)(2,1)S(1)}) fusion(s32[8,32]{1,0:T(8,128)} %param.15), kind=kLoop, calls=%fused_computation.180 | loop fusion | flops 256 | bytes 2048 | tf_op jit(solution)/shard_map/broadcast_in_dim | solution.py:331
  0.8 0.9 %copy.136 = bf16[8,32,128]{2,0,1:T(8,128)(2,1)S(1)} copy(bf16[8,32,128]{2,1,0:T(8,128)(2,1)} %param.14) | data formatting | bytes 131072 | tf_op args[0]
  1.9 0.8 %copy-done.3 = bf16[8,32,128]{2,1,0:T(8,128)(2,1)S(1)} copy-done((bf16[8,32,128]{2,1,0:T(8,128)(2,1)S(1)}, bf16[8,32,128]{2,1,0:T(8,128)(2,1)}, u32[]{:S(2)}) %copy-start.3) | copy-done | bytes 65560
  2.8 11.6 %shard_map.136 = (bf16[4,192,128]{2,1,0:T(8,128)(2,1)S(1)}, bf16[8,96,128]{2,1,0:T(8,128)(2,1)S(1)}, bf16[8,48,128]{2,1,0:T(8,128)(2,1)S(1)}, bf16[16,16,128]{2,1,0:T(8,128)(2,1)S(1)}) custom-call(bf16[4,192,128]{2,1,0:T(8,128)(2,1)S(1)} %pad_maximum_fusion.4.refs_0_, bf16[8,96,128]{2,1,0:T(8,128)(2,1)S(1)} %bitcast_dynamic-update-slice_fusion.refs_1_, ...), custom_call_target="tpu_custom_call" | custom-call | tf_op jit(solution)/shard_map/pallas_call | solution.py:149
  15.1 0.6 %copy-done.14 = f32[128]{0:T(128)S(1)} copy-done((f32[128]{0:T(128)S(1)}, f32[128]{0:T(128)}, u32[]{:S(2)}) %copy-start.14) | copy-done | bytes 536
  15.9 0.7 %copy-done.8 = bf16[128,512]{1,0:T(8,128)(2,1)S(1)} copy-done((bf16[128,512]{1,0:T(8,128)(2,1)S(1)}, bf16[128,512]{1,0:T(8,128)(2,1)}, u32[]{:S(2)}) %copy-start.8) | copy-done | bytes 131096
  16.9 0.7 %copy-done.13 = f32[3,3,256]{2,1,0:T(4,128)S(1)} copy-done((f32[3,3,256]{2,1,0:T(4,128)S(1)}, f32[3,3,256]{2,1,0:T(4,128)}, u32[]{:S(2)}) %copy-start.13) | copy-done | bytes 9240
  17.6 0.7 %copy-done.17 = f32[256]{0:T(256)S(1)} copy-done((f32[256]{0:T(256)S(1)}, f32[256]{0:T(256)}, u32[]{:S(2)}) %copy-start.17) | copy-done | bytes 1048
  20.6 0.9 %broadcast_multiply_fusion = (f32[2,4,64,256]{3,2,1,0:T(8,128)S(1)}, f32[2,4,64,256]{3,2,1,0:T(8,128)S(1)}) fusion(f32[4,64,256]{2,1,0:T(8,128)S(1)} %get-tuple-element.21, f32[4,64,256]{2,1,0:T(8,128)S(1)} %fusion.29, f32[2,256]{1,0:T(2,128)S(1)} %get-tuple-element.87, f32[4,8,256]{2,1,0:T(8,128)S(1)} %copy-done.12, f32[4,64,2,40]{1,3,2,0:T(8,128)S(1)} %fusion.49), kind=kOutput, calls=%fused_computation.69 | convolution fusion | flops 13762560 | bytes 1624064 | tf_op jit(solution)/shard_map/pqdr,dre->dpqe/dot_general | solution.py:276
  23.5 1.0 %fusion.75 = (f32[2,128,256]{2,1,0:T(8,128)}, bf16[2,128,256]{2,1,0:T(8,128)(2,1)S(1)}) fusion(f32[256]{0:T(256)S(1)} %bitcast.379, f32[256]{0:T(256)S(1)} %bitcast.372, bf16[2,128,256]{2,1,0:T(8,128)(2,1)S(1)} %bitcast.336, f32[256]{0:T(256)S(1)} %bitcast.373, f32[256]{0:T(256)S(1)} %bitcast.374, f32[256]{0:T(256)S(1)} %bitcast.375, ...), kind=kLoop, calls=%fused_computation.187 | loop fusion | flops 2162688 | bytes 1058816 | tf_op jit(solution)/shard_map/convert_element_type | solution.py:267
  26.6 0.9 %broadcast_multiply_fusion.1 = (f32[2,2,128,256]{3,2,1,0:T(8,128)S(1)}, f32[2,2,128,256]{3,2,1,0:T(8,128)S(1)}) fusion(f32[2,128,256]{2,1,0:T(8,128)S(1)} %copy-done.6, f32[2,128,256]{2,1,0:T(8,128)S(1)} %fusion.31, f32[2,256]{1,0:T(2,128)S(1)} %get-tuple-element.88, f32[4,8,256]{2,1,0:T(8,128)S(1)} %copy-done.12, f32[2,128,2,40]{1,3,2,0:T(8,128)S(1)} %fusion.51), kind=kOutput, calls=%fused_computation.72 | convolution fusion | flops 13762560 | bytes 1607680 | tf_op jit(solution)/shard_map/pqdr,dre->dpqe/dot_general | solution.py:276
  27.5 0.9 %fusion.78 = (f32[1,2,128,256]{3,2,1,0:T(8,128)}, f32[2,128,256]{2,1,0:T(8,128)S(1)}, f32[2,128,256]{2,1,0:T(8,128)S(1)}, f32[1,2,128,256]{3,2,1,0:T(8,128)}) fusion(f32[2,2,128,256]{3,2,1,0:T(8,128)S(1)} %get-tuple-element.93, f32[2,2,128,256]{3,2,1,0:T(8,128)S(1)} %get-tuple-element.94), kind=kLoop, calls=%fused_computation.190 | loop fusion | bytes 2097152 | tf_op jit(solution)/shard_map/slice | solution.py:240
  28.8 1.1 %stack.107 = f32[1,2,128,2,128]{4,3,2,1,0:T(2,128)S(1)} reshape(f32[1,2,128,256]{3,2,1,0:T(8,128)} %get-tuple-element.29) | data formatting | bytes 524288 | tf_op jit(solution)/shard_map/stack | solution.py:240
  30.7 0.9 %copy.75 = f32[1,2,128,2,128]{4,1,0,3,2:T(2,128)} copy(f32[1,2,128,2,128]{4,3,2,1,0:T(2,128)S(1)} %stack.105) | data formatting | bytes 524288 | tf_op jit(solution)/shard_map/stack | solution.py:240
  31.6 1.1 %stack.104 = f32[1,2,128,2,128]{4,3,2,1,0:T(2,128)S(1)} reshape(f32[1,2,128,256]{3,2,1,0:T(8,128)} %get-tuple-element.98) | data formatting | bytes 524288 | tf_op jit(solution)/shard_map/stack | solution.py:240
  32.9 0.7 %copy-done.7 = f32[1,2,128,2,128]{4,1,0,3,2:T(2,128)S(1)} copy-done((f32[1,2,128,2,128]{4,1,0,3,2:T(2,128)S(1)}, f32[1,2,128,2,128]{4,1,0,3,2:T(2,128)}, u32[]{:S(2)}) %copy-start.7) | copy-done | bytes 262168
  34.5 0.7 %broadcast_in_dim.28 = f32[16,2,4,256]{3,2,1,0:T(4,128)} broadcast(f32[16,2,256]{2,1,0:T(2,128)S(1)} %copy.88), dimensions={0,1,3} | broadcast | bytes 163840 | tf_op jit(solution)/shard_map/broadcast_in_dim | solution.py:291
  35.2 0.9 %broadcast_in_dim.29.rate_c = f32[16,8,256]{2,1,0:T(8,128)S(1)} reshape(f32[16,2,4,256]{3,2,1,0:T(4,128)} %broadcast_in_dim.28) | data formatting | bytes 262144 | tf_op jit(solution)/shard_map/broadcast_in_dim | solution.py:291
  36.2 10.3 %shard_map.137 = (f32[128,8,128]{2,1,0:T(8,128)S(1)}, f32[64,8,256]{2,1,0:T(8,128)S(1)}) custom-call(f32[128,8,128]{2,1,0:T(8,128)S(1)} %bitcast.298, f32[128,8,128]{2,1,0:T(8,128)S(1)} %bitcast.297, f32[1024,32]{1,0:T(8,128)S(1)} %bitcast.296, f32[16,8,128]{2,1,0:T(8,128)S(1)} %bitcast.306, f32[64,8,256]{2,1,0:T(8,128)S(1)} %copy.100.step_c, ...), custom_call_target="tpu_custom_call" | custom-call | tf_op jit(solution)/shard_map/pallas_call | solution.py:214
  48.1 1.0 %copy-done.2 = f32[128,8,128]{2,1,0:T(8,128)S(1)} copy-done((f32[128,8,128]{2,1,0:T(8,128)S(1)}, f32[128,8,128]{2,1,0:T(8,128)}, u32[]{:S(2)}) %copy-start.2) | copy-done | bytes 524312
  49.7 0.7 %copy-done.5 = bf16[2,128,256]{2,1,0:T(8,128)(2,1)S(1)} copy-done((bf16[2,128,256]{2,1,0:T(8,128)(2,1)S(1)}, bf16[2,128,256]{2,1,0:T(8,128)(2,1)}, u32[]{:S(2)}) %copy-start.5) | copy-done | bytes 131096
  50.4 7.8 %shard_map.138 = (bf16[4,64,256]{2,1,0:T(8,128)(2,1)S(1)}, bf16[8,32,256]{2,1,0:T(8,128)(2,1)S(1)}) custom-call(bf16[4,64,256]{2,1,0:T(8,128)(2,1)S(1)} %bitcast.305, bf16[8,32,256]{2,1,0:T(8,128)(2,1)S(1)} %copy_bitcast_fusion.1.refs_1_), custom_call_target="tpu_custom_call" | custom-call | tf_op jit(solution)/shard_map/pallas_call | solution.py:149
  59.9 0.7 %copy-done.18 = bf16[256,128]{1,0:T(8,128)(2,1)S(1)} copy-done((bf16[256,128]{1,0:T(8,128)(2,1)S(1)}, bf16[256,128]{1,0:T(8,128)(2,1)}, u32[]{:S(2)}) %copy-start.18) | copy-done | bytes 65560
  60.6 0.9 %fusion.2 = bf16[8,32,128]{2,1,0:T(8,128)(2,1)} fusion(bf16[8,32,128]{2,1,0:T(8,128)(2,1)S(1)} %copy-done.3, bf16[8,32,256]{2,1,0:T(8,128)(2,1)S(1)} %bitcast.348, f32[256]{0:T(256)S(1)} %copy-done.19, f32[8,32]{1,0:T(8,128)S(1)} %add_rsqrt_fusion.1, f32[8,32]{1,0:T(8,128)S(1)} %broadcast_multiply_fusion.3, bf16[8,32,256]{2,1,0:T(8,128)(2,1)S(1)} %bitcast.302, ...), kind=kOutput, calls=%fused_computation.10 | convolution fusion | flops 17661952 | bytes 723968 | tf_op jit(solution)/shard_map/dot_general | solution.py:396
  (143 shorter events, 13.4 us)
Async XLA Ops:
  0.0 19.8 %copy-start = (f32[256,256]{1,0:T(8,128)S(1)}, f32[256,256]{1,0:T(8,128)}, u32[]{:S(2)}) copy-start(f32[256,256]{1,0:T(8,128)} %param.23) | copy-start | bytes 786436
  1.9 0.8 %copy-start.3 = (bf16[8,32,128]{2,1,0:T(8,128)(2,1)S(1)}, bf16[8,32,128]{2,1,0:T(8,128)(2,1)}, u32[]{:S(2)}) copy-start(bf16[8,32,128]{2,1,0:T(8,128)(2,1)} %param.14) | copy-start | bytes 196612
  15.1 0.7 %copy-start.14 = (f32[128]{0:T(128)S(1)}, f32[128]{0:T(128)}, u32[]{:S(2)}) copy-start(f32[128]{0:T(128)} %param.16) | copy-start | bytes 1540
  15.8 0.9 %copy-start.8 = (bf16[128,512]{1,0:T(8,128)(2,1)S(1)}, bf16[128,512]{1,0:T(8,128)(2,1)}, u32[]{:S(2)}) copy-start(bf16[128,512]{1,0:T(8,128)(2,1)} %param.17) | copy-start | bytes 393220
  16.9 0.7 %copy-start.13 = (f32[3,3,256]{2,1,0:T(4,128)S(1)}, f32[3,3,256]{2,1,0:T(4,128)}, u32[]{:S(2)}) copy-start(f32[3,3,256]{2,1,0:T(4,128)} %param.18) | copy-start | bytes 27652
  17.6 0.7 %copy-start.17 = (f32[256]{0:T(256)S(1)}, f32[256]{0:T(256)}, u32[]{:S(2)}) copy-start(f32[256]{0:T(256)} %param.19) | copy-start | bytes 3076
  18.3 0.9 %copy-start.10 = (bf16[256,160]{0,1:T(8,128)(2,1)S(1)}, bf16[256,160]{0,1:T(8,128)(2,1)}, u32[]{:S(2)}) copy-start(bf16[256,160]{0,1:T(8,128)(2,1)} %param.20) | copy-start | bytes 245764
  19.8 0.7 %copy-start.16 = (f32[4,256]{1,0:T(4,128)S(1)}, f32[4,256]{1,0:T(4,128)}, u32[]{:S(2)}) copy-start(f32[4,256]{1,0:T(4,128)} %param.22) | copy-start | bytes 12292
  19.8 0.8 %copy-start.12 = (f32[4,8,256]{2,1,0:T(8,128)S(1)}, f32[4,8,256]{2,1,0:T(8,128)}, u32[]{:S(2)}) copy-start(f32[4,8,256]{2,1,0:T(8,128)} %param.21) | copy-start | bytes 98308
  24.5 0.7 %copy-start.4 = (bf16[2,128,256]{2,1,0:T(8,128)(2,1)}, bf16[2,128,256]{2,1,0:T(8,128)(2,1)S(1)}, u32[]{:S(2)}) copy-start(bf16[2,128,256]{2,1,0:T(8,128)(2,1)S(1)} %get-tuple-element.24) | copy-start | bytes 393220
  25.6 1.0 %copy-start.6 = (f32[2,128,256]{2,1,0:T(8,128)S(1)}, f32[2,128,256]{2,1,0:T(8,128)}, u32[]{:S(2)}) copy-start(f32[2,128,256]{2,1,0:T(8,128)} %get-tuple-element.23) | copy-start | bytes 786436
  32.7 1.0 %copy-start.7 = (f32[1,2,128,2,128]{4,1,0,3,2:T(2,128)S(1)}, f32[1,2,128,2,128]{4,1,0,3,2:T(2,128)}, u32[]{:S(2)}) copy-start(f32[1,2,128,2,128]{4,1,0,3,2:T(2,128)} %copy.75) | copy-start | bytes 786436
  33.6 0.8 %copy-start.11 = (f32[4,16,256]{2,1,0:T(8,128)S(1)}, f32[4,16,256]{2,1,0:T(8,128)}, u32[]{:S(2)}) copy-start(f32[4,16,256]{2,1,0:T(8,128)} %param.24) | copy-start | bytes 196612
  46.5 0.8 %copy-start.1 = (f32[128,8,128]{2,1,0:T(8,128)}, f32[128,8,128]{2,1,0:T(8,128)S(1)}, u32[]{:S(2)}) copy-start(f32[128,8,128]{2,1,0:T(8,128)S(1)} %get-tuple-element.17) | copy-start | bytes 1572868
  47.4 0.7 %copy-start.15 = (f32[4,256]{1,0:T(4,128)S(1)}, f32[4,256]{1,0:T(4,128)}, u32[]{:S(2)}) copy-start(f32[4,256]{1,0:T(4,128)} %param.25) | copy-start | bytes 12292
  48.0 1.0 %copy-start.2 = (f32[128,8,128]{2,1,0:T(8,128)S(1)}, f32[128,8,128]{2,1,0:T(8,128)}, u32[]{:S(2)}) copy-start(f32[128,8,128]{2,1,0:T(8,128)} %copy-done.1) | copy-start | bytes 1572868
  49.5 0.9 %copy-start.5 = (bf16[2,128,256]{2,1,0:T(8,128)(2,1)S(1)}, bf16[2,128,256]{2,1,0:T(8,128)(2,1)}, u32[]{:S(2)}) copy-start(bf16[2,128,256]{2,1,0:T(8,128)(2,1)} %copy-done.4) | copy-start | bytes 393220
  58.8 0.9 %copy-start.9 = (bf16[128,512]{1,0:T(8,128)(2,1)S(1)}, bf16[128,512]{1,0:T(8,128)(2,1)}, u32[]{:S(2)}) copy-start(bf16[128,512]{1,0:T(8,128)(2,1)} %param.17) | copy-start | bytes 393220
  59.7 0.8 %copy-start.18 = (bf16[256,128]{1,0:T(8,128)(2,1)S(1)}, bf16[256,128]{1,0:T(8,128)(2,1)}, u32[]{:S(2)}) copy-start(bf16[256,128]{1,0:T(8,128)(2,1)} %param.27) | copy-start | bytes 196612
  59.9 0.7 %copy-start.19 = (f32[256]{0:T(256)S(1)}, f32[256]{0:T(256)}, u32[]{:S(2)}) copy-start(f32[256]{0:T(256)} %param.26) | copy-start | bytes 3076

commit v2 on v1

--- a/solution.py
+++ b/solution.py
@@ -158,148 +158,203 @@
     )(*args)
 
 
-def scan_kernel(
-    states, chunk, step_r, drive_r, coef_r, rate_r, step_c, drive_c, coef_c, rate_c, y_r, y_c, pick, wide, state_ref
+def to_eight(count):
+    return -(-count // 8) * 8
+
+
+def strip_kernel(
+    states, low_rank, chunk,
+    feats_r, codes_r, feats_c, codes_c,
+    norm_gain, in_weight, conv_weight, conv_bias, proj, step_weight, step_bias, code_table,
+    decay_rates, skip_gain,
+    y_r, y_c,
+    pick, wide, state_ref, inner_r, inner_c, sig_r, sig_c, step_r, step_c, drive_r, drive_c,
+    coef_r, coef_c, rate_r, rate_c, out_r, out_c,
 ):
     place = lax.broadcasted_iota(jnp.int32, pick.shape, 0)
     lane = lax.broadcasted_iota(jnp.int32, pick.shape, 1)
     pick[...] = jnp.where(lax.rem(place, 2 * states) == lane // LANES, 1.0, 0.0).astype(jnp.bfloat16)
-
-    def run(step, drive, coef, rate, out):
-        length, lines, lanes = step.shape
-        copies = lanes // LANES
+    inner_width = code_table.shape[1]
+    halves = inner_width // LANES
+    exact = lax.Precision.HIGHEST
+
+    def run(feats, codes, inner_ref, sig, step, drive, coef, rate, out, y, first):
+        lines, length = feats.shape[0] - 2, feats.shape[1]
+        copies = step.shape[0]
+        inside = halves // copies
+        used = inside * 2 * lines
+        rows = step.shape[1] // length
+        if used < rows:
+            for ref in (step, drive, coef, rate):
+                ref[...] = jnp.zeros_like(ref)
+        inner_ref[:, :8, :] = jnp.zeros((lines + 2, 8, inner_width), jnp.float32)
+        inner_ref[:, 8 + length :, :] = jnp.zeros((lines + 2, 8, inner_width), jnp.float32)
+        for line in range(lines + 2):
+            normed = layer_norm(feats[line].astype(jnp.float32), norm_gain[...])
+            inner = jnp.dot(
+                normed.astype(jnp.bfloat16),
+                in_weight[:, :inner_width],
+                preferred_element_type=jnp.float32,
+            )
+            inner_ref[line, 8 : 8 + length, :] = inner.astype(jnp.bfloat16).astype(jnp.float32)
+        at_row = lax.broadcasted_iota(jnp.int32, (length, length), 0)
+        at_col = lax.broadcasted_iota(jnp.int32, (length, length), 1)
+        turn = jnp.where(at_row + at_col == length - 1, 1.0, 0.0)
+
+        def slots(line, d, half):
+            part, inner_half = half % copies, half // copies
+            return part, (inner_half * 2 + d) * lines + line
+
+        for d in range(2):
+            for half in range(halves):
+                for line in range(lines):
+                    part, slot = slots(line, d, half)
+                    rate[part, pl.ds(slot, states, stride=rows), :] = decay_rates[
+                        first + d, :, half * LANES : (half + 1) * LANES
+                    ] * (-1.0 / math.log(2.0))
+        for line in range(lines):
+            summed = jnp.zeros((length, inner_width), jnp.float32) + conv_bias[...]
+            for i in range(3):
+                for j in range(3):
+                    tap = i * 3 + j if first == 0 else j * 3 + i
+                    summed = summed + (
+                        inner_ref[line + i, 7 + j : 7 + j + length, :] * conv_weight[tap : tap + 1, :]
+                    )
+            signal_low = jax.nn.silu(summed).astype(jnp.bfloat16)
+            signal = signal_low.astype(jnp.float32)
+            sig[line] = signal
+            hot = codes[line * length : (line + 1) * length, :] == lax.broadcasted_iota(
+                jnp.int32, (length, code_table.shape[0]), 1
+            )
+            offsets = jnp.dot(
+                jnp.where(hot, 1.0, 0.0), code_table[...],
+                precision=exact, preferred_element_type=jnp.float32,
+            )
+            for d in range(2):
+                way = first + d
+                mix = jnp.dot(
+                    signal_low,
+                    proj[:, way * LANES : (way + 1) * LANES],
+                    preferred_element_type=jnp.float32,
+                )
+                raw = (
+                    jnp.dot(
+                        mix[:, 2 * states : 2 * states + low_rank],
+                        step_weight[way],
+                        precision=exact,
+                        preferred_element_type=jnp.float32,
+                    )
+                    + step_bias[way : way + 1, :]
+                    + offsets
+                )
+                size = jnp.maximum(raw, 0.0) + jnp.log1p(jnp.exp(-jnp.abs(raw)))
+                push = size * signal
+                if d == 1:
+                    size, push, mix = (
+                        jnp.dot(turn, v, precision=exact, preferred_element_type=jnp.float32)
+                        for v in (size, push, mix)
+                    )
+                for half in range(halves):
+                    part, slot = slots(line, d, half)
+                    at = pl.ds(slot, length, stride=rows)
+                    step[part, at, :] = size[:, half * LANES : (half + 1) * LANES]
+                    drive[part, at, :] = push[:, half * LANES : (half + 1) * LANES]
+                    if part == 0:
+                        coef[at, :] = mix
+
         state_ref[...] = jnp.zeros_like(state_ref)
 
         @pl.loop(0, length // chunk)
         def _(block):
-            rows = chunk * lines
-            values = coef[pl.ds(pl.multiple_of(block * rows, rows), rows), :]
+            span = chunk * rows
+            values = coef[pl.ds(pl.multiple_of(block * span, span), span), :][:, : 2 * states]
             high = values.astype(jnp.bfloat16)
             rest = values - high.astype(jnp.float32)
             middle = rest.astype(jnp.bfloat16)
             low = (rest - middle.astype(jnp.float32)).astype(jnp.bfloat16)
             parts = jnp.concatenate([high, middle, low], axis=1)
-            wide[...] = jnp.dot(parts, pick[...], preferred_element_type=jnp.float32)
+            wide[:span, :] = jnp.dot(parts, pick[...], preferred_element_type=jnp.float32)
 
             def advance(k, state):
-                t = block * chunk + k
-                at = pl.ds(pl.multiple_of(k * lines, lines), lines)
-                size, push = step[t], drive[t]
-                new, sums = [], [None, None]
+                at = pl.ds(pl.multiple_of(k * rows, rows), rows)
+                now_at = pl.ds(pl.multiple_of((block * chunk + k) * rows, rows), rows)
+                size = [step[p, now_at, :] for p in range(copies)]
+                push = [drive[p, now_at, :] for p in range(copies)]
+                new = []
+                sums = [[None, None] for _ in range(copies)]
                 for n in range(states):
                     into = wide[at, n * LANES : (n + 1) * LANES]
                     outof = wide[at, (states + n) * LANES : (states + n + 1) * LANES]
-                    if copies > 1:
-                        into = jnp.concatenate([into] * copies, axis=1)
-                        outof = jnp.concatenate([outof] * copies, axis=1)
-                    now = jnp.exp2(size * rate[n]) * state[n] + push * into
-                    new.append(now)
-                    term = now * outof
-                    sums[n % 2] = term if sums[n % 2] is None else sums[n % 2] + term
-                out[t] = sums[0] + sums[1]
+                    for p in range(copies):
+                        decay = jnp.exp2(size[p] * rate[p, n * rows : (n + 1) * rows, :])
+                        now = decay * state[n * copies + p] + push[p] * into
+                        new.append(now)
+                        term = now * outof
+                        old = sums[p][n % 2]
+                        sums[p][n % 2] = term if old is None else old + term
+                for p in range(copies):
+                    out[p, now_at, :] = sums[p][0] + sums[p][1]
                 return tuple(new)
 
-            start = tuple(state_ref[n, :, :lanes] for n in range(states))
+            start = tuple(state_ref[k, :rows, :] for k in range(states * copies))
             end = lax.fori_loop(0, chunk, advance, start, unroll=4)
-            for n in range(states):
-                state_ref[n, :, :lanes] = end[n]
-
-    run(step_r, drive_r, coef_r, rate_r, y_r)
-    run(step_c, drive_c, coef_c, rate_c, y_c)
-
-
-def scans(row_args, col_args, states):
-    lines = row_args[0].shape[1]
-    chunk = math.gcd(16, math.gcd(row_args[0].shape[0], col_args[0].shape[0]))
+            for k in range(states * copies):
+                state_ref[k, :rows, :] = end[k]
+
+        direct = skip_gain[first : first + 1, :] + skip_gain[first + 1 : first + 2, :]
+        for line in range(lines):
+            for half in range(halves):
+                lanes = slice(half * LANES, (half + 1) * LANES)
+                part, slot = slots(line, 0, half)
+                forward = out[part, pl.ds(slot, length, stride=rows), :]
+                part, slot = slots(line, 1, half)
+                back = jnp.dot(
+                    turn,
+                    out[part, pl.ds(slot, length, stride=rows), :],
+                    precision=exact,
+                    preferred_element_type=jnp.float32,
+                )
+                total = forward + back + direct[:, lanes] * sig[line, :, lanes]
+                y[line, :, lanes] = total.astype(jnp.bfloat16)
+
+    run(feats_r, codes_r, inner_r, sig_r, step_r, drive_r, coef_r, rate_r, out_r, y_r, 0)
+    run(feats_c, codes_c, inner_c, sig_c, step_c, drive_c, coef_c, rate_c, out_c, y_c, 2)
+
+
+def strips(feats_r, codes_r, feats_c, codes_c, weights, states, low_rank):
+    inner_width = weights[1].shape[1] // 2
+    halves = inner_width // LANES
+    lengths = [feats_r.shape[1], feats_c.shape[1]]
+    lines = [feats_r.shape[0] - 2, feats_c.shape[0] - 2]
+    copies = [1, halves]
+    rows = [to_eight(halves // c * 2 * n) for c, n in zip(copies, lines)]
+    chunk = math.gcd(16, math.gcd(*lengths))
+
+    def pair(shape):
+        return [pltpu.VMEM(shape(lines[k], lengths[k], copies[k], rows[k]), jnp.float32) for k in (0, 1)]
+
+    args = (feats_r, codes_r, feats_c, codes_c) + weights
     return pl.pallas_call(
-        functools.partial(scan_kernel, states, chunk),
-        out_shape=(
-            jax.ShapeDtypeStruct(row_args[0].shape, jnp.float32),
-            jax.ShapeDtypeStruct(col_args[0].shape, jnp.float32),
+        functools.partial(strip_kernel, states, low_rank, chunk),
+        out_shape=tuple(
+            jax.ShapeDtypeStruct((lines[k], lengths[k], inner_width), jnp.bfloat16) for k in (0, 1)
         ),
-        in_specs=[pl.BlockSpec(memory_space=pltpu.VMEM)] * 8,
+        in_specs=[pl.BlockSpec(memory_space=pltpu.VMEM)] * len(args),
         out_specs=(pl.BlockSpec(memory_space=pltpu.VMEM),) * 2,
         scratch_shapes=[
             pltpu.VMEM((6 * states, 2 * states * LANES), jnp.bfloat16),
-            pltpu.VMEM((chunk * lines, 2 * states * LANES), jnp.float32),
-            pltpu.VMEM((states, lines, max(row_args[0].shape[2], col_args[0].shape[2])), jnp.float32),
+            pltpu.VMEM((chunk * max(rows), 2 * states * LANES), jnp.float32),
+            pltpu.VMEM((states * halves, max(rows), LANES), jnp.float32),
+            *pair(lambda n, t, c, r: (n + 2, t + 16, inner_width)),
+            *pair(lambda n, t, c, r: (n, t, inner_width)),
+            *pair(lambda n, t, c, r: (c, t * r, LANES)),
+            *pair(lambda n, t, c, r: (c, t * r, LANES)),
+            *pair(lambda n, t, c, r: (t * r, LANES)),
+            *pair(lambda n, t, c, r: (c, states * r, LANES)),
+            *pair(lambda n, t, c, r: (c, t * r, LANES)),
         ],
-        compiler_params=pltpu.CompilerParams(vmem_limit_bytes=32 * 2**20),
-    )(*row_args, *col_args)
-
-
-def to_tile(values, axis):
-    pads = [(0, 0)] * values.ndim
-    pads[axis] = (0, -values.shape[axis] % 8)
-    return jnp.pad(values, pads)
-
-
-def fold(values, lanes):
-    _, lines, length, channels = values.shape
-    parts = channels // lanes
-    flipped = jnp.stack([values[0], jnp.flip(values[1], 1)])
-    split = flipped.reshape(2, lines, length, parts, lanes)
-    return to_tile(split.transpose(2, 3, 0, 1, 4).reshape(length, parts * 2 * lines, lanes), 1)
-
-
-def strip_inputs(feats, codes, conv, weights, first, lanes):
-    (norm_gain, in_weight, conv_bias, proj_weight, step_weight, step_bias, code_table, decay_rates) = weights
-    lines, length = codes.shape
-    inner_width = in_weight.shape[1] // 2
-    states, low_rank = decay_rates.shape[1], step_weight.shape[1]
-    halves = inner_width // lanes
-    wide = low_rank + 2 * states
-    normed = layer_norm(feats.astype(jnp.float32), norm_gain).astype(jnp.bfloat16)
-    inner = jnp.dot(
-        normed.reshape(-1, feats.shape[2]),
-        in_weight[:, :inner_width],
-        preferred_element_type=jnp.float32,
-    ).astype(jnp.bfloat16)
-    inner = inner.reshape(lines + 2, length, inner_width)
-    padded = jnp.pad(inner, ((0, 0), (1, 1), (0, 0)))
-    summed = jnp.zeros((lines, length, inner_width), jnp.float32) + conv_bias
-    for a in range(3):
-        for b in range(3):
-            summed = (
-                summed + padded[a : a + lines, b : b + length].astype(jnp.float32) * conv[a, b]
-            )
-    signal_low = jax.nn.silu(summed).astype(jnp.bfloat16)
-    signal = signal_low.astype(jnp.float32)
-    coefs = jnp.dot(
-        signal_low.reshape(-1, inner_width),
-        proj_weight[:, first * wide : (first + 2) * wide],
-        preferred_element_type=jnp.float32,
-    ).reshape(lines, length, 2, wide)
-    one_hot = (codes[:, :, None] == jnp.arange(code_table.shape[0])).astype(jnp.float32)
-    offsets = jnp.einsum("pqk,ke->pqe", one_hot, code_table, precision=lax.Precision.HIGHEST)
-    step = jax.nn.softplus(
-        jnp.einsum(
-            "pqdr,dre->dpqe",
-            coefs[..., :low_rank],
-            step_weight[first : first + 2],
-            precision=lax.Precision.HIGHEST,
-        )
-        + step_bias[first : first + 2, None, None, :]
-        + offsets
-    )
-    mix = coefs[..., low_rank:].transpose(2, 0, 1, 3)
-    mix = jnp.stack([mix[0], jnp.flip(mix[1], 1)]).transpose(2, 0, 1, 3)
-    mix = mix.reshape(length, 1, 2 * lines, 2 * states)
-    mix = jnp.broadcast_to(mix, (length, halves, 2 * lines, 2 * states))
-    mix = to_tile(mix.reshape(length, halves * 2 * lines, 2 * states), 1).reshape(-1, 2 * states)
-    rate = (decay_rates[first : first + 2] * (-1.0 / math.log(2.0))).reshape(2, states, halves, lanes)
-    rate = jnp.broadcast_to(
-        rate.transpose(1, 2, 0, 3)[:, :, :, None, :], (states, halves, 2, lines, lanes)
-    ).reshape(states, halves * 2 * lines, lanes)
-    return (fold(step, lanes), fold(step * signal, lanes), mix, to_tile(rate, 1)), signal
-
-
-def unfold(y, lines, channels):
-    length, _, lanes = y.shape
-    parts = channels // lanes
-    y = y[:, : parts * 2 * lines].reshape(length, parts, 2, lines, lanes)
-    y = y[:, :, 0] + jnp.flip(y[:, :, 1], 0)
-    return y.transpose(2, 0, 1, 3).reshape(lines, length, channels)
+        compiler_params=pltpu.CompilerParams(vmem_limit_bytes=40 * 2**20),
+    )(*args)
 
 
 def on_device(
@@ -363,8 +418,13 @@
         )
         return feats.reshape(lines + 2, parts * length, width), code.astype(jnp.int32)
 
+    low_rank = step_weight.shape[1]
+    proj = proj_weight.reshape(inner_width, -1, low_rank + 2 * states)
+    proj = jnp.concatenate([proj[..., low_rank:], proj[..., :low_rank]], axis=-1)
+    proj = jnp.pad(proj, ((0, 0), (0, 0), (0, LANES - low_rank - 2 * states)))
     weights = (
-        norm_gain, in_weight, conv_bias, proj_weight, step_weight, step_bias, code_table, decay_rates,
+        norm_gain[None, :], in_weight, conv_weight.reshape(9, inner_width), conv_bias[None, :],
+        proj.reshape(inner_width, -1), step_weight, step_bias, code_table, decay_rates, skip_gain,
     )
     feats_r, codes_r = assembled(
         got_r, halo_r, nx, rp, row_size, cols, place_x, place_y, nx, ny
@@ -372,13 +432,11 @@
     feats_c, codes_c = assembled(
         got_c, halo_c, ny, cp, col_size, rows, place_y, place_x, ny, nx
     )
-    row_args, signal_r = strip_inputs(feats_r, codes_r, conv_weight, weights, 0, LANES)
-    col_args, signal_c = strip_inputs(feats_c, codes_c, jnp.swapaxes(conv_weight, 0, 1), weights, 2, inner_width)
-    y_r, y_c = scans(row_args, col_args, states)
-    y_r = unfold(y_r, rp, inner_width) + (skip_gain[0] + skip_gain[1]) * signal_r
-    y_c = unfold(y_c, cp, inner_width) + (skip_gain[2] + skip_gain[3]) * signal_c
-    y_r = y_r.astype(jnp.bfloat16).reshape(rp, nx, cols, inner_width).transpose(1, 0, 2, 3)
-    y_c = y_c.astype(jnp.bfloat16).reshape(cp, ny, rows, inner_width).transpose(1, 0, 2, 3)
+    y_r, y_c = strips(
+        feats_r, codes_r.reshape(-1, 1), feats_c, codes_c.reshape(-1, 1), weights, states, low_rank
+    )
+    y_r = y_r.reshape(rp, nx, cols, inner_width).transpose(1, 0, 2, 3)
+    y_c = y_c.reshape(cp, ny, rows, inner_width).transpose(1, 0, 2, 3)
     back_r, back_c = exchange(
         y_r.reshape(nx, rp * cols, inner_width), y_c.reshape(ny, cp * rows, inner_width), 1
     )

time: 62.3 us -> 46.2 us (0.74)
  local copies, waits for them, and re-layouts: 21.7 us -> 5.01 us
  Pallas kernels: 29.8 us -> 37.6 us
  other arithmetic: 4.96 us -> 1.7 us
  matrix products: 4.31 us -> 1.09 us
    pallas_call x1, Pallas kernels: 10.3 us -> 18.2 us  [strips(): pl.pallas_call(functools.partial(strip_kernel, states, low_rank, chunk),...]
    unnamed x50 -> x34, local copies, waits for them, and re-layouts: 12 us -> 4.37 us
    another operation x8 -> x0, local copies, waits for them, and re-layouts: 3.95 us -> none  [fold(): flipped = jnp.stack([values[0], jnp.flip(values[1], 1)])]
    dot_general x8 -> x0, matrix products: 3.2 us -> none  [the longest x2 1.83 us: strip_inputs(): jnp.einsum('pqdr,dre->dpqe', coefs[..., :low_rank], step_weight[first:fir...]
    broadcast_in_dim x6 -> x0, local copies, waits for them, and re-layouts: 1.89 us -> none  [the longest x4 1.67 us: strip_inputs(): jnp.broadcast_to(rate.transpose(1, 2, 0, 3)[:, :, :, None, :], (states, h...]
    convert_element_type x7 -> x0, other arithmetic: 1.78 us -> none  [the longest x2 1.33 us: strip_inputs(): signal = signal_low.astype(jnp.float32)]
    slice x8 -> x2, local copies, waits for them, and re-layouts: 1.06 us -> 0.01 us  [the longest x1 0.01 us: on_device(): proj[..., low_rank:]]
    reshape x6 -> x4, local copies, waits for them, and re-layouts: 1.03 us -> 0.17 us  [the longest x1 0.14 us: on_device(): proj.reshape(inner_width, -1)]
where the time goes in v2:
time: 46.2 us; the launch traced here: 45.9 us
  Pallas kernels  37.6 us (81%)
  local copies, waits for them, and re-layouts  5.01 us (11%)
  other arithmetic  1.7 us (4%)
  matrix products  1.09 us (2%)
  between operations  0.48 us (1%)
    pallas_call x2, Pallas kernels, exchange(): pl.pallas_call(functools.partial(exchange_kernel, nx, ny, edges is not No...  19.4 us
    pallas_call x1, Pallas kernels, strips(): pl.pallas_call(functools.partial(strip_kernel, states, low_rank, chunk),...  18.2 us
    unnamed x34, local copies, waits for them, and re-layouts  4.37 us

profile of v2, /device:TPU:0, one launch (start us, length us, event | category | flops | bytes accessed | tf_op | source)
XLA Modules:
  0.0 45.9 jit_solution(1475671344020566634)
XLA Ops:
  0.0 0.7 %convert_bitcast_fusion.2 = (bf16[32,1,8]{0,2,1:T(8,128)(2,1)S(1)}, bf16[8,1,32]{2,0,1:T(8,128)(2,1)S(1)}) fusion(s32[8,32]{1,0:T(8,128)} %param.15), kind=kLoop, calls=%fused_computation.72 | loop fusion | flops 256 | bytes 2048 | tf_op jit(solution)/shard_map/broadcast_in_dim | solution.py:386
  0.7 0.1 copy.56
  0.8 0.9 %copy.90 = bf16[8,32,128]{2,0,1:T(8,128)(2,1)S(1)} copy(bf16[8,32,128]{2,1,0:T(8,128)(2,1)} %param.14) | data formatting | bytes 131072 | tf_op args[0]
  1.9 0.8 %copy-done.9 = bf16[8,32,128]{2,1,0:T(8,128)(2,1)S(1)} copy-done((bf16[8,32,128]{2,1,0:T(8,128)(2,1)S(1)}, bf16[8,32,128]{2,1,0:T(8,128)(2,1)}, u32[]{:S(2)}) %copy-start.9) | copy-done | bytes 65560
  2.8 11.6 %shard_map.136 = (bf16[4,192,128]{2,1,0:T(8,128)(2,1)S(1)}, bf16[8,96,128]{2,1,0:T(8,128)(2,1)S(1)}, bf16[8,48,128]{2,1,0:T(8,128)(2,1)S(1)}, bf16[16,16,128]{2,1,0:T(8,128)(2,1)S(1)}) custom-call(bf16[4,192,128]{2,1,0:T(8,128)(2,1)S(1)} %pad_maximum_fusion.refs_0_, bf16[8,96,128]{2,1,0:T(8,128)(2,1)S(1)} %bitcast_dynamic-update-slice_fusion.refs_1_, ...), custom_call_target="tpu_custom_call" | custom-call | tf_op jit(solution)/shard_map/pallas_call | solution.py:149
  14.7 0.1 reshape.170.codes_c
  14.8 0.1 reshape.169.codes_r
  15.0 0.7 %copy-done.10 = bf16[256,160]{0,1:T(8,128)(2,1)S(1)} copy-done((bf16[256,160]{0,1:T(8,128)(2,1)S(1)}, bf16[256,160]{0,1:T(8,128)(2,1)}, u32[]{:S(2)}) %copy-start.10) | copy-done | bytes 81944
  15.8 0.1 copy.67.proj
  15.9 0.5 %copy-done.11 = f32[3,3,256]{2,1,0:T(4,128)S(1)} copy-done((f32[3,3,256]{2,1,0:T(4,128)S(1)}, f32[3,3,256]{2,1,0:T(4,128)}, u32[]{:S(2)}) %copy-start.11) | copy-done | bytes 9240
  16.5 0.2 copy-done.1
  16.6 0.1 copy-done.2
  16.8 0.4 copy-done.5
  17.2 0.0 copy-done.8
  17.2 18.2 %shard_map.137 = (bf16[2,128,256]{2,1,0:T(8,128)(2,1)S(1)}, bf16[4,64,256]{2,1,0:T(8,128)(2,1)S(1)}) custom-call(bf16[4,128,128]{2,1,0:T(8,128)(2,1)S(1)} %pad_maximum_fusion.1.feats_r, s32[256,1]{1,0:T(8,128)S(1)} %reshape.169.codes_r, bf16[6,64,128]{2,1,0:T(8,128)(2,1)S(1)} %pad_maximum_fusion.2.feats_c, s32[256,1]{1,0:T(8,128)S(1)} %reshape.170.codes_c, ...), custom_call_target="tpu_custom_call" | custom-call | tf_op jit(solution)/shard_map/pallas_call | solution.py:337
  35.4 7.8 %shard_map.138 = (bf16[4,64,256]{2,1,0:T(8,128)(2,1)S(1)}, bf16[8,32,256]{2,1,0:T(8,128)(2,1)S(1)}) custom-call(bf16[4,64,256]{2,1,0:T(8,128)(2,1)S(1)} %bitcast.106, bf16[8,32,256]{2,1,0:T(8,128)(2,1)S(1)} %copy_bitcast_fusion.1.refs_1_), custom_call_target="tpu_custom_call" | custom-call | tf_op jit(solution)/shard_map/pallas_call | solution.py:149
  43.3 0.2 fusion.19
  43.5 0.2 multiply_reduce_fusion
  43.7 0.1 convert_reduce_fusion
  43.8 0.2 fusion.13
  44.0 0.1 fusion.15
  44.1 0.2 convolution_convert_fusion
  44.3 0.7 %copy-done.12 = f32[256]{0:T(256)S(1)} copy-done((f32[256]{0:T(256)S(1)}, f32[256]{0:T(256)}, u32[]{:S(2)}) %copy-start.12) | copy-done | bytes 1048
  45.0 0.9 %fusion = bf16[8,32,128]{2,1,0:T(8,128)(2,1)} fusion(bf16[8,32,128]{2,1,0:T(8,128)(2,1)S(1)} %copy-done.9, bf16[8,32,256]{2,1,0:T(8,128)(2,1)S(1)} %bitcast.125, f32[256]{0:T(256)S(1)} %copy-done.12, f32[8,32]{1,0:T(8,128)S(1)} %add_rsqrt_fusion.1, f32[8,32]{1,0:T(8,128)S(1)} %broadcast_multiply_fusion.1, bf16[8,32,256]{2,1,0:T(8,128)(2,1)S(1)} %bitcast.105, ...), kind=kOutput, calls=%fused_computation.2 | convolution fusion | flops 17661952 | bytes 723968 | tf_op jit(solution)/shard_map/dot_general | solution.py:454
  (59 shorter events, 0.5 us)
Async XLA Ops:
  0.0 44.3 %copy-start = (bf16[256,128]{1,0:T(8,128)(2,1)S(1)}, bf16[256,128]{1,0:T(8,128)(2,1)}, u32[]{:S(2)}) copy-start(bf16[256,128]{1,0:T(8,128)(2,1)} %param.27) | copy-start | bytes 196612
  1.9 0.8 %copy-start.9 = (bf16[8,32,128]{2,1,0:T(8,128)(2,1)S(1)}, bf16[8,32,128]{2,1,0:T(8,128)(2,1)}, u32[]{:S(2)}) copy-start(bf16[8,32,128]{2,1,0:T(8,128)(2,1)} %param.14) | copy-start | bytes 196612
  14.8 0.9 %copy-start.10 = (bf16[256,160]{0,1:T(8,128)(2,1)S(1)}, bf16[256,160]{0,1:T(8,128)(2,1)}, u32[]{:S(2)}) copy-start(bf16[256,160]{0,1:T(8,128)(2,1)} %param.20) | copy-start | bytes 245764
  15.7 0.7 %copy-start.11 = (f32[3,3,256]{2,1,0:T(4,128)S(1)}, f32[3,3,256]{2,1,0:T(4,128)}, u32[]{:S(2)}) copy-start(f32[3,3,256]{2,1,0:T(4,128)} %param.18) | copy-start | bytes 27652
  15.7 0.9 %copy-start.1 = (bf16[128,512]{1,0:T(8,128)(2,1)S(1)}, bf16[128,512]{1,0:T(8,128)(2,1)}, u32[]{:S(2)}) copy-start(bf16[128,512]{1,0:T(8,128)(2,1)} %in_weight.1) | copy-start | bytes 393220
  15.7 1.0 %copy-start.2 = (f32[256,256]{1,0:T(8,128)S(1)}, f32[256,256]{1,0:T(8,128)}, u32[]{:S(2)}) copy-start(f32[256,256]{1,0:T(8,128)} %code_table.1) | copy-start | bytes 786436
  15.8 1.0 %copy-start.3 = (f32[4,16,256]{2,1,0:T(8,128)S(1)}, f32[4,16,256]{2,1,0:T(8,128)}, u32[]{:S(2)}) copy-start(f32[4,16,256]{2,1,0:T(8,128)} %decay_rates.1) | copy-start | bytes 196612
  15.8 1.0 %copy-start.4 = (f32[4,8,256]{2,1,0:T(8,128)S(1)}, f32[4,8,256]{2,1,0:T(8,128)}, u32[]{:S(2)}) copy-start(f32[4,8,256]{2,1,0:T(8,128)} %step_weight.1) | copy-start | bytes 98308
  16.4 0.7 %copy-start.5 = (f32[4,256]{1,0:T(4,128)S(1)}, f32[4,256]{1,0:T(4,128)}, u32[]{:S(2)}) copy-start(f32[4,256]{1,0:T(4,128)} %step_bias.1) | copy-start | bytes 12292
  16.4 0.7 %copy-start.6 = (f32[4,256]{1,0:T(4,128)S(1)}, f32[4,256]{1,0:T(4,128)}, u32[]{:S(2)}) copy-start(f32[4,256]{1,0:T(4,128)} %skip_gain.1) | copy-start | bytes 12292
  16.4 0.7 %copy-start.7 = (f32[128]{0:T(128)S(1)}, f32[128]{0:T(128)}, u32[]{:S(2)}) copy-start(f32[128]{0:T(128)} %param.16) | copy-start | bytes 1540
  16.5 0.7 %copy-start.8 = (f32[256]{0:T(256)S(1)}, f32[256]{0:T(256)}, u32[]{:S(2)}) copy-start(f32[256]{0:T(256)} %param.19) | copy-start | bytes 3076
  44.3 0.7 %copy-start.12 = (f32[256]{0:T(256)S(1)}, f32[256]{0:T(256)}, u32[]{:S(2)}) copy-start(f32[256]{0:T(256)} %param.26) | copy-start | bytes 3076

commit v3 on v2

--- a/solution.py
+++ b/solution.py
@@ -162,6 +162,15 @@
     return -(-count // 8) * 8
 
 
+def chosen(picks, values):
+    high = values.astype(jnp.bfloat16)
+    rest = values - high.astype(jnp.float32)
+    middle = rest.astype(jnp.bfloat16)
+    low = (rest - middle.astype(jnp.float32)).astype(jnp.bfloat16)
+    out = [jnp.dot(picks, part, preferred_element_type=jnp.float32) for part in (low, middle, high)]
+    return (out[0] + out[1]) + out[2]
+
+
 def strip_kernel(
     states, low_rank, chunk,
     feats_r, codes_r, feats_c, codes_c,
@@ -199,7 +208,13 @@
             inner_ref[line, 8 : 8 + length, :] = inner.astype(jnp.bfloat16).astype(jnp.float32)
         at_row = lax.broadcasted_iota(jnp.int32, (length, length), 0)
         at_col = lax.broadcasted_iota(jnp.int32, (length, length), 1)
-        turn = jnp.where(at_row + at_col == length - 1, 1.0, 0.0)
+        turn = jnp.where(at_row + at_col == length - 1, 1.0, 0.0).astype(jnp.bfloat16)
+        hot = codes[...] == lax.broadcasted_iota(
+            jnp.int32, (lines * length, code_table.shape[0]), 1
+        )
+        all_offsets = chosen(jnp.where(hot, 1.0, 0.0).astype(jnp.bfloat16), code_table[...])
+        slot_at = lax.broadcasted_iota(jnp.int32, (rows, LANES), 0)
+        ahead = lax.rem(slot_at // lines, 2) == 0
 
         def slots(line, d, half):
             part, inner_half = half % copies, half // copies
@@ -223,13 +238,7 @@
             signal_low = jax.nn.silu(summed).astype(jnp.bfloat16)
             signal = signal_low.astype(jnp.float32)
             sig[line] = signal
-            hot = codes[line * length : (line + 1) * length, :] == lax.broadcasted_iota(
-                jnp.int32, (length, code_table.shape[0]), 1
-            )
-            offsets = jnp.dot(
-                jnp.where(hot, 1.0, 0.0), code_table[...],
-                precision=exact, preferred_element_type=jnp.float32,
-            )
+            offsets = all_offsets[line * length : (line + 1) * length, :]
             for d in range(2):
                 way = first + d
                 mix = jnp.dot(
@@ -250,10 +259,7 @@
                 size = jnp.maximum(raw, 0.0) + jnp.log1p(jnp.exp(-jnp.abs(raw)))
                 push = size * signal
                 if d == 1:
-                    size, push, mix = (
-                        jnp.dot(turn, v, precision=exact, preferred_element_type=jnp.float32)
-                        for v in (size, push, mix)
-                    )
+                    mix = chosen(turn, mix)
                 for half in range(halves):
                     part, slot = slots(line, d, half)
                     at = pl.ds(slot, length, stride=rows)
@@ -278,8 +284,13 @@
             def advance(k, state):
                 at = pl.ds(pl.multiple_of(k * rows, rows), rows)
                 now_at = pl.ds(pl.multiple_of((block * chunk + k) * rows, rows), rows)
-                size = [step[p, now_at, :] for p in range(copies)]
-                push = [drive[p, now_at, :] for p in range(copies)]
+                last_at = pl.ds(
+                    pl.multiple_of((length - 1 - block * chunk - k) * rows, rows), rows
+                )
+                size, push = (
+                    [jnp.where(ahead, ref[p, now_at, :], ref[p, last_at, :]) for p in range(copies)]
+                    for ref in (step, drive)
+                )
                 new = []
                 sums = [[None, None] for _ in range(copies)]
                 for n in range(states):
@@ -294,6 +305,7 @@
                         sums[p][n % 2] = term if old is None else old + term
                 for p in range(copies):
                     out[p, now_at, :] = sums[p][0] + sums[p][1]
+                    out[copies + p, last_at, :] = sums[p][0] + sums[p][1]
                 return tuple(new)
 
             start = tuple(state_ref[k, :rows, :] for k in range(states * copies))
@@ -308,12 +320,7 @@
                 part, slot = slots(line, 0, half)
                 forward = out[part, pl.ds(slot, length, stride=rows), :]
                 part, slot = slots(line, 1, half)
-                back = jnp.dot(
-                    turn,
-                    out[part, pl.ds(slot, length, stride=rows), :],
-                    precision=exact,
-                    preferred_element_type=jnp.float32,
-                )
+                back = out[copies + part, pl.ds(slot, length, stride=rows), :]
                 total = forward + back + direct[:, lanes] * sig[line, :, lanes]
                 y[line, :, lanes] = total.astype(jnp.bfloat16)
 
@@ -351,7 +358,7 @@
             *pair(lambda n, t, c, r: (c, t * r, LANES)),
             *pair(lambda n, t, c, r: (t * r, LANES)),
             *pair(lambda n, t, c, r: (c, states * r, LANES)),
-            *pair(lambda n, t, c, r: (c, t * r, LANES)),
+            *pair(lambda n, t, c, r: (2 * c, t * r, LANES)),
         ],
         compiler_params=pltpu.CompilerParams(vmem_limit_bytes=40 * 2**20),
     )(*args)

time: 46.2 us -> 42.6 us (0.922)
  Pallas kernels: 37.6 us -> 34 us
    pallas_call x1, Pallas kernels: 18.2 us -> 14.6 us  [strips(): pl.pallas_call(functools.partial(strip_kernel, states, low_rank, chunk),...]
where the time goes in v3:
time: 42.6 us; the launch traced here: 42.3 us
  Pallas kernels  34 us (80%)
  local copies, waits for them, and re-layouts  5.01 us (12%)
  other arithmetic  1.7 us (4%)
  matrix products  1.09 us (3%)
  between operations  0.48 us (1%)
    pallas_call x2, Pallas kernels, exchange(): pl.pallas_call(functools.partial(exchange_kernel, nx, ny, edges is not No...  19.4 us
    pallas_call x1, Pallas kernels, strips(): pl.pallas_call(functools.partial(strip_kernel, states, low_rank, chunk),...  14.6 us
    unnamed x34, local copies, waits for them, and re-layouts  4.37 us
    dot_general x1, matrix products, on_device(): jnp.dot(mixed.reshape(-1, inner_width), out_weight, preferred_element_typ...  0.92 us

profile of v3, /device:TPU:0, one launch (start us, length us, event | category | flops | bytes accessed | tf_op | source)
XLA Modules:
  0.0 42.3 jit_solution(13623186929428893889)
XLA Ops:
  0.0 0.7 %convert_bitcast_fusion.2 = (bf16[32,1,8]{0,2,1:T(8,128)(2,1)S(1)}, bf16[8,1,32]{2,0,1:T(8,128)(2,1)S(1)}) fusion(s32[8,32]{1,0:T(8,128)} %param.15), kind=kLoop, calls=%fused_computation.72 | loop fusion | flops 256 | bytes 2048 | tf_op jit(solution)/shard_map/broadcast_in_dim | solution.py:393
  0.7 0.1 copy.56
  0.8 0.9 %copy.90 = bf16[8,32,128]{2,0,1:T(8,128)(2,1)S(1)} copy(bf16[8,32,128]{2,1,0:T(8,128)(2,1)} %param.14) | data formatting | bytes 131072 | tf_op args[0]
  1.9 0.8 %copy-done.9 = bf16[8,32,128]{2,1,0:T(8,128)(2,1)S(1)} copy-done((bf16[8,32,128]{2,1,0:T(8,128)(2,1)S(1)}, bf16[8,32,128]{2,1,0:T(8,128)(2,1)}, u32[]{:S(2)}) %copy-start.9) | copy-done | bytes 65560
  2.8 11.6 %shard_map.136 = (bf16[4,192,128]{2,1,0:T(8,128)(2,1)S(1)}, bf16[8,96,128]{2,1,0:T(8,128)(2,1)S(1)}, bf16[8,48,128]{2,1,0:T(8,128)(2,1)S(1)}, bf16[16,16,128]{2,1,0:T(8,128)(2,1)S(1)}) custom-call(bf16[4,192,128]{2,1,0:T(8,128)(2,1)S(1)} %pad_maximum_fusion.refs_0_, bf16[8,96,128]{2,1,0:T(8,128)(2,1)S(1)} %bitcast_dynamic-update-slice_fusion.refs_1_, ...), custom_call_target="tpu_custom_call" | custom-call | tf_op jit(solution)/shard_map/pallas_call | solution.py:149
  14.7 0.1 reshape.170.codes_c
  14.8 0.1 reshape.169.codes_r
  15.0 0.7 %copy-done.10 = bf16[256,160]{0,1:T(8,128)(2,1)S(1)} copy-done((bf16[256,160]{0,1:T(8,128)(2,1)S(1)}, bf16[256,160]{0,1:T(8,128)(2,1)}, u32[]{:S(2)}) %copy-start.10) | copy-done | bytes 81944
  15.8 0.1 copy.67.proj
  15.9 0.5 %copy-done.11 = f32[3,3,256]{2,1,0:T(4,128)S(1)} copy-done((f32[3,3,256]{2,1,0:T(4,128)S(1)}, f32[3,3,256]{2,1,0:T(4,128)}, u32[]{:S(2)}) %copy-start.11) | copy-done | bytes 9240
  16.5 0.2 copy-done.1
  16.6 0.1 copy-done.2
  16.8 0.4 copy-done.5
  17.2 0.0 copy-done.8
  17.2 14.6 %shard_map.137 = (bf16[2,128,256]{2,1,0:T(8,128)(2,1)S(1)}, bf16[4,64,256]{2,1,0:T(8,128)(2,1)S(1)}) custom-call(bf16[4,128,128]{2,1,0:T(8,128)(2,1)S(1)} %pad_maximum_fusion.1.feats_r, s32[256,1]{1,0:T(8,128)S(1)} %reshape.169.codes_r, bf16[6,64,128]{2,1,0:T(8,128)(2,1)S(1)} %pad_maximum_fusion.2.feats_c, s32[256,1]{1,0:T(8,128)S(1)} %reshape.170.codes_c, ...), custom_call_target="tpu_custom_call" | custom-call | tf_op jit(solution)/shard_map/pallas_call | solution.py:344
  31.8 7.8 %shard_map.138 = (bf16[4,64,256]{2,1,0:T(8,128)(2,1)S(1)}, bf16[8,32,256]{2,1,0:T(8,128)(2,1)S(1)}) custom-call(bf16[4,64,256]{2,1,0:T(8,128)(2,1)S(1)} %bitcast.106, bf16[8,32,256]{2,1,0:T(8,128)(2,1)S(1)} %copy_bitcast_fusion.1.refs_1_), custom_call_target="tpu_custom_call" | custom-call | tf_op jit(solution)/shard_map/pallas_call | solution.py:149
  39.7 0.2 fusion.19
  39.9 0.2 multiply_reduce_fusion
  40.1 0.1 convert_reduce_fusion
  40.2 0.2 fusion.13
  40.4 0.1 fusion.15
  40.5 0.2 convolution_convert_fusion
  40.7 0.7 %copy-done.12 = f32[256]{0:T(256)S(1)} copy-done((f32[256]{0:T(256)S(1)}, f32[256]{0:T(256)}, u32[]{:S(2)}) %copy-start.12) | copy-done | bytes 1048
  41.4 0.9 %fusion = bf16[8,32,128]{2,1,0:T(8,128)(2,1)} fusion(bf16[8,32,128]{2,1,0:T(8,128)(2,1)S(1)} %copy-done.9, bf16[8,32,256]{2,1,0:T(8,128)(2,1)S(1)} %bitcast.125, f32[256]{0:T(256)S(1)} %copy-done.12, f32[8,32]{1,0:T(8,128)S(1)} %add_rsqrt_fusion.1, f32[8,32]{1,0:T(8,128)S(1)} %broadcast_multiply_fusion.1, bf16[8,32,256]{2,1,0:T(8,128)(2,1)S(1)} %bitcast.105, ...), kind=kOutput, calls=%fused_computation.2 | convolution fusion | flops 17661952 | bytes 723968 | tf_op jit(solution)/shard_map/dot_general | solution.py:461
  (59 shorter events, 0.5 us)
Async XLA Ops:
  0.0 40.7 %copy-start = (bf16[256,128]{1,0:T(8,128)(2,1)S(1)}, bf16[256,128]{1,0:T(8,128)(2,1)}, u32[]{:S(2)}) copy-start(bf16[256,128]{1,0:T(8,128)(2,1)} %param.27) | copy-start | bytes 196612
  1.9 0.8 %copy-start.9 = (bf16[8,32,128]{2,1,0:T(8,128)(2,1)S(1)}, bf16[8,32,128]{2,1,0:T(8,128)(2,1)}, u32[]{:S(2)}) copy-start(bf16[8,32,128]{2,1,0:T(8,128)(2,1)} %param.14) | copy-start | bytes 196612
  14.8 0.9 %copy-start.10 = (bf16[256,160]{0,1:T(8,128)(2,1)S(1)}, bf16[256,160]{0,1:T(8,128)(2,1)}, u32[]{:S(2)}) copy-start(bf16[256,160]{0,1:T(8,128)(2,1)} %param.20) | copy-start | bytes 245764
  15.7 0.7 %copy-start.11 = (f32[3,3,256]{2,1,0:T(4,128)S(1)}, f32[3,3,256]{2,1,0:T(4,128)}, u32[]{:S(2)}) copy-start(f32[3,3,256]{2,1,0:T(4,128)} %param.18) | copy-start | bytes 27652
  15.7 0.9 %copy-start.1 = (bf16[128,512]{1,0:T(8,128)(2,1)S(1)}, bf16[128,512]{1,0:T(8,128)(2,1)}, u32[]{:S(2)}) copy-start(bf16[128,512]{1,0:T(8,128)(2,1)} %in_weight.1) | copy-start | bytes 393220
  15.7 1.0 %copy-start.2 = (f32[256,256]{1,0:T(8,128)S(1)}, f32[256,256]{1,0:T(8,128)}, u32[]{:S(2)}) copy-start(f32[256,256]{1,0:T(8,128)} %code_table.1) | copy-start | bytes 786436
  15.8 1.0 %copy-start.3 = (f32[4,16,256]{2,1,0:T(8,128)S(1)}, f32[4,16,256]{2,1,0:T(8,128)}, u32[]{:S(2)}) copy-start(f32[4,16,256]{2,1,0:T(8,128)} %decay_rates.1) | copy-start | bytes 196612
  15.8 1.0 %copy-start.4 = (f32[4,8,256]{2,1,0:T(8,128)S(1)}, f32[4,8,256]{2,1,0:T(8,128)}, u32[]{:S(2)}) copy-start(f32[4,8,256]{2,1,0:T(8,128)} %step_weight.1) | copy-start | bytes 98308
  16.4 0.7 %copy-start.5 = (f32[4,256]{1,0:T(4,128)S(1)}, f32[4,256]{1,0:T(4,128)}, u32[]{:S(2)}) copy-start(f32[4,256]{1,0:T(4,128)} %step_bias.1) | copy-start | bytes 12292
  16.4 0.7 %copy-start.6 = (f32[4,256]{1,0:T(4,128)S(1)}, f32[4,256]{1,0:T(4,128)}, u32[]{:S(2)}) copy-start(f32[4,256]{1,0:T(4,128)} %skip_gain.1) | copy-start | bytes 12292
  16.4 0.7 %copy-start.7 = (f32[128]{0:T(128)S(1)}, f32[128]{0:T(128)}, u32[]{:S(2)}) copy-start(f32[128]{0:T(128)} %param.16) | copy-start | bytes 1540
  16.5 0.7 %copy-start.8 = (f32[256]{0:T(256)S(1)}, f32[256]{0:T(256)}, u32[]{:S(2)}) copy-start(f32[256]{0:T(256)} %param.19) | copy-start | bytes 3076
  40.7 0.7 %copy-start.12 = (f32[256]{0:T(256)S(1)}, f32[256]{0:T(256)}, u32[]{:S(2)}) copy-start(f32[256]{0:T(256)} %param.26) | copy-start | bytes 3076

commit v4 on v3

--- a/solution.py
+++ b/solution.py
@@ -387,33 +387,40 @@
     rp, cp = rows // nx, cols // ny
     codes = scene_codes.astype(jnp.bfloat16)
 
-    def payload(block, code):
-        lines, length, _ = block.shape
-        size = -(-(length + 1) // 16) * 16
-        code = jnp.pad(code[:, None, :], ((0, 0), (0, size - length - 1), (0, width - length)))
-        return jnp.concatenate([block, code], axis=1)
-
-    row_load = payload(features, codes)
-    col_load = payload(jnp.swapaxes(features, 0, 1), codes.T)
-    row_size, col_size = row_load.shape[1], col_load.shape[1]
-    edges = tuple(jnp.stack([load[0], load[-1]]) for load in (row_load, col_load))
-    row_load, col_load = (jnp.pad(load, ((1, 1), (0, 0), (0, 0))) for load in (row_load, col_load))
-    xr = jnp.stack([row_load[k * rp : k * rp + rp + 2] for k in range(nx)])
-    xc = jnp.stack([col_load[k * cp : k * cp + cp + 2] for k in range(ny)])
-    got_r, got_c, halo_r, halo_c = exchange(
-        xr.reshape(nx, (rp + 2) * row_size, width),
-        xc.reshape(ny, (cp + 2) * col_size, width),
-        0,
-        edges,
-    )
+    def to_sixteen(count):
+        return -(-count // 16) * 16
+
+    def payload(block, code, lines, parts):
+        length = block.shape[1]
+        padded = jnp.pad(block, ((1, 1), (0, 0), (0, 0)))
+        code = jnp.pad(code, ((0, 0), (0, width - length)))
+        count = (lines + 2) * length + lines
+        rest = jnp.zeros((to_sixteen(count) - count, width), block.dtype)
+        slots = [
+            jnp.concatenate(
+                [
+                    padded[k * lines : (k + 1) * lines + 2].reshape(-1, width),
+                    code[k * lines : (k + 1) * lines],
+                    rest,
+                ]
+            )
+            for k in range(parts)
+        ]
+        edge = jnp.stack([block[0], block[-1]])
+        return jnp.stack(slots), jnp.pad(edge, ((0, 0), (0, to_sixteen(length) - length), (0, 0)))
+
+    xr, edge_r = payload(features, codes, rp, nx)
+    xc, edge_c = payload(jnp.swapaxes(features, 0, 1), codes.T, cp, ny)
+    got_r, got_c, halo_r, halo_c = exchange(xr, xc, 0, (edge_r, edge_c))
     place_x, place_y = lax.axis_index("gx"), lax.axis_index("gy")
 
-    def assembled(got, halo, parts, lines, size, length, inner, outer, inner_count, outer_count):
-        got = got.reshape(parts, lines + 2, size, width)
-        code = got[:, 1:-1, length, :length].transpose(1, 0, 2).reshape(lines, parts * length)
-        feats = got[:, :, :length].transpose(1, 0, 2, 3)
+    def assembled(got, halo, parts, lines, length, inner, outer, inner_count, outer_count):
+        count = (lines + 2) * length
+        code = got[:, count : count + lines, :length]
+        code = code.transpose(1, 0, 2).reshape(lines, parts * length)
+        feats = got[:, :count].reshape(parts, lines + 2, length, width).transpose(1, 0, 2, 3)
         none = jnp.zeros_like(feats[0])
-        halo = halo.reshape(2, parts, size, width)
+        halo = halo.reshape(2, parts, -1, width)
         before = jnp.where(outer > 0, halo[0, :, :length], none)
         after = jnp.where(outer < outer_count - 1, halo[1, :, :length], none)
         feats = jnp.concatenate(
@@ -434,10 +441,10 @@
         proj.reshape(inner_width, -1), step_weight, step_bias, code_table, decay_rates, skip_gain,
     )
     feats_r, codes_r = assembled(
-        got_r, halo_r, nx, rp, row_size, cols, place_x, place_y, nx, ny
+        got_r, halo_r, nx, rp, cols, place_x, place_y, nx, ny
     )
     feats_c, codes_c = assembled(
-        got_c, halo_c, ny, cp, col_size, rows, place_y, place_x, ny, nx
+        got_c, halo_c, ny, cp, rows, place_y, place_x, ny, nx
     )
     y_r, y_c = strips(
         feats_r, codes_r.reshape(-1, 1), feats_c, codes_c.reshape(-1, 1), weights, states, low_rank

time: 42.6 us -> 42.2 us (level)
  Pallas kernels: 34 us -> 32.7 us
  local copies, waits for them, and re-layouts: 5.01 us -> 5.87 us
    pallas_call x2, Pallas kernels: 19.4 us -> 18.1 us  [exchange(): pl.pallas_call(functools.partial(exchange_kernel, nx, ny, edges is not No...]
    broadcast_in_dim x1 -> x0, other arithmetic: 0.72 us -> none  [payload(): code[:, None, :]]
    unnamed x0 -> x7, other arithmetic: none -> 0.59 us
    unnamed x34 -> x30, local copies, waits for them, and re-layouts: 4.37 us -> 4.77 us
where the time goes in v4:
time: 42.2 us; the launch traced here: 41.9 us
  Pallas kernels  32.7 us (77%)
  local copies, waits for them, and re-layouts  5.87 us (14%)
  other arithmetic  1.7 us (4%)
  matrix products  1.09 us (3%)
  between operations  0.49 us (1%)
    pallas_call x2, Pallas kernels, exchange(): pl.pallas_call(functools.partial(exchange_kernel, nx, ny, edges is not No...  18.1 us
    pallas_call x1, Pallas kernels, strips(): pl.pallas_call(functools.partial(strip_kernel, states, low_rank, chunk),...  14.6 us
    unnamed x30, local copies, waits for them, and re-layouts  4.77 us
    dot_general x1, matrix products, on_device(): jnp.dot(mixed.reshape(-1, inner_width), out_weight, preferred_element_typ...  0.92 us

profile of v4, /device:TPU:0, one launch (start us, length us, event | category | flops | bytes accessed | tf_op | source)
XLA Modules:
  0.0 41.9 jit_solution(7140656825406342184)
XLA Ops:
  0.0 0.9 %copy.76 = bf16[8,32,128]{2,0,1:T(8,128)(2,1)S(1)} copy(bf16[8,32,128]{2,1,0:T(8,128)(2,1)} %param.14) | data formatting | bytes 131072 | tf_op args[0]
  0.9 0.7 %copy-done.12 = s32[8,32]{1,0:T(8,128)S(1)} copy-done((s32[8,32]{1,0:T(8,128)S(1)}, s32[8,32]{1,0:T(8,128)}, u32[]{:S(2)}) %copy-start.12) | copy-done | bytes 1048
  2.7 0.1 copy.49
  2.8 0.1 copy.50
  2.9 0.5 %copy-done.9 = bf16[8,32,128]{2,1,0:T(8,128)(2,1)S(1)} copy-done((bf16[8,32,128]{2,1,0:T(8,128)(2,1)S(1)}, bf16[8,32,128]{2,1,0:T(8,128)(2,1)}, u32[]{:S(2)}) %copy-start.9) | copy-done | bytes 65560
  3.5 0.1 maximum_bitcast_fusion
  3.7 10.6 %shard_map.136 = (bf16[4,144,128]{2,1,0:T(8,128)(2,1)S(1)}, bf16[8,64,128]{2,1,0:T(8,128)(2,1)S(1)}, bf16[8,32,128]{2,1,0:T(8,128)(2,1)S(1)}, bf16[16,16,128]{2,1,0:T(8,128)(2,1)S(1)}) custom-call(bf16[4,144,128]{2,1,0:T(8,128)(2,1)S(1)} %pad_maximum_fusion.refs_0_, bf16[8,64,128]{2,1,0:T(8,128)(2,1)S(1)} %constant_dynamic-update-slice_fusion.refs_1_, ...), custom_call_target="tpu_custom_call" | custom-call | tf_op jit(solution)/shard_map/pallas_call | solution.py:149
  14.7 0.1 reshape.190.codes_r
  14.8 0.7 %copy-done.10 = bf16[256,160]{0,1:T(8,128)(2,1)S(1)} copy-done((bf16[256,160]{0,1:T(8,128)(2,1)S(1)}, bf16[256,160]{0,1:T(8,128)(2,1)}, u32[]{:S(2)}) %copy-start.10) | copy-done | bytes 81944
  15.6 0.1 copy.62.proj
  15.8 0.5 %copy-done.11 = f32[3,3,256]{2,1,0:T(4,128)S(1)} copy-done((f32[3,3,256]{2,1,0:T(4,128)S(1)}, f32[3,3,256]{2,1,0:T(4,128)}, u32[]{:S(2)}) %copy-start.11) | copy-done | bytes 9240
  16.3 0.2 copy-done.1
  16.5 0.1 copy-done.2
  16.6 0.4 copy-done.5
  17.1 14.6 %shard_map.137 = (bf16[2,128,256]{2,1,0:T(8,128)(2,1)S(1)}, bf16[4,64,256]{2,1,0:T(8,128)(2,1)S(1)}) custom-call(bf16[4,128,128]{2,1,0:T(8,128)(2,1)S(1)} %pad_maximum_fusion.1.feats_r, s32[256,1]{1,0:T(8,128)S(1)} %reshape.190.codes_r, bf16[6,64,128]{2,1,0:T(8,128)(2,1)S(1)} %pad_maximum_fusion.2.feats_c, s32[256,1]{1,0:T(8,128)S(1)} %reshape.191.codes_c, ...), custom_call_target="tpu_custom_call" | custom-call | tf_op jit(solution)/shard_map/pallas_call | solution.py:344
  31.7 7.5 %shard_map.138 = (bf16[4,64,256]{2,1,0:T(8,128)(2,1)S(1)}, bf16[8,32,256]{2,1,0:T(8,128)(2,1)S(1)}) custom-call(bf16[4,64,256]{2,1,0:T(8,128)(2,1)S(1)} %bitcast.130, bf16[8,32,256]{2,1,0:T(8,128)(2,1)S(1)} %copy_bitcast_fusion.refs_1_), custom_call_target="tpu_custom_call" | custom-call | tf_op jit(solution)/shard_map/pallas_call | solution.py:149
  39.2 0.2 fusion.15
  39.4 0.2 multiply_reduce_fusion
  39.6 0.1 convert_reduce_fusion
  39.7 0.2 fusion.11
  39.9 0.1 fusion.13
  40.1 0.2 convolution_convert_fusion
  40.3 0.7 %copy-done.13 = f32[256]{0:T(256)S(1)} copy-done((f32[256]{0:T(256)S(1)}, f32[256]{0:T(256)}, u32[]{:S(2)}) %copy-start.13) | copy-done | bytes 1048
  40.9 0.9 %fusion = bf16[8,32,128]{2,1,0:T(8,128)(2,1)} fusion(bf16[8,32,128]{2,1,0:T(8,128)(2,1)S(1)} %copy-done.9, bf16[8,32,256]{2,1,0:T(8,128)(2,1)S(1)} %bitcast.144, f32[256]{0:T(256)S(1)} %copy-done.13, f32[8,32]{1,0:T(8,128)S(1)} %add_rsqrt_fusion.1, f32[8,32]{1,0:T(8,128)S(1)} %broadcast_multiply_fusion.1, bf16[8,32,256]{2,1,0:T(8,128)(2,1)S(1)} %bitcast.129, ...), kind=kOutput, calls=%fused_computation.2 | convolution fusion | flops 17661952 | bytes 723968 | tf_op jit(solution)/shard_map/dot_general | solution.py:468
  (71 shorter events, 1.7 us)
Async XLA Ops:
  0.0 40.3 %copy-start = (bf16[256,128]{1,0:T(8,128)(2,1)S(1)}, bf16[256,128]{1,0:T(8,128)(2,1)}, u32[]{:S(2)}) copy-start(bf16[256,128]{1,0:T(8,128)(2,1)} %param.27) | copy-start | bytes 196612
  0.9 0.7 %copy-start.12 = (s32[8,32]{1,0:T(8,128)S(1)}, s32[8,32]{1,0:T(8,128)}, u32[]{:S(2)}) copy-start(s32[8,32]{1,0:T(8,128)} %param.15) | copy-start | bytes 3076
  2.6 0.8 %copy-start.9 = (bf16[8,32,128]{2,1,0:T(8,128)(2,1)S(1)}, bf16[8,32,128]{2,1,0:T(8,128)(2,1)}, u32[]{:S(2)}) copy-start(bf16[8,32,128]{2,1,0:T(8,128)(2,1)} %param.14) | copy-start | bytes 196612
  14.7 0.9 %copy-start.10 = (bf16[256,160]{0,1:T(8,128)(2,1)S(1)}, bf16[256,160]{0,1:T(8,128)(2,1)}, u32[]{:S(2)}) copy-start(bf16[256,160]{0,1:T(8,128)(2,1)} %param.20) | copy-start | bytes 245764
  15.6 0.7 %copy-start.11 = (f32[3,3,256]{2,1,0:T(4,128)S(1)}, f32[3,3,256]{2,1,0:T(4,128)}, u32[]{:S(2)}) copy-start(f32[3,3,256]{2,1,0:T(4,128)} %param.18) | copy-start | bytes 27652
  15.6 0.9 %copy-start.1 = (bf16[128,512]{1,0:T(8,128)(2,1)S(1)}, bf16[128,512]{1,0:T(8,128)(2,1)}, u32[]{:S(2)}) copy-start(bf16[128,512]{1,0:T(8,128)(2,1)} %in_weight.1) | copy-start | bytes 393220
  15.6 1.0 %copy-start.2 = (f32[256,256]{1,0:T(8,128)S(1)}, f32[256,256]{1,0:T(8,128)}, u32[]{:S(2)}) copy-start(f32[256,256]{1,0:T(8,128)} %code_table.1) | copy-start | bytes 786436
  15.6 1.0 %copy-start.3 = (f32[4,16,256]{2,1,0:T(8,128)S(1)}, f32[4,16,256]{2,1,0:T(8,128)}, u32[]{:S(2)}) copy-start(f32[4,16,256]{2,1,0:T(8,128)} %decay_rates.1) | copy-start | bytes 196612
  15.6 1.0 %copy-start.4 = (f32[4,8,256]{2,1,0:T(8,128)S(1)}, f32[4,8,256]{2,1,0:T(8,128)}, u32[]{:S(2)}) copy-start(f32[4,8,256]{2,1,0:T(8,128)} %step_weight.1) | copy-start | bytes 98308
  16.3 0.7 %copy-start.5 = (f32[4,256]{1,0:T(4,128)S(1)}, f32[4,256]{1,0:T(4,128)}, u32[]{:S(2)}) copy-start(f32[4,256]{1,0:T(4,128)} %step_bias.1) | copy-start | bytes 12292
  16.3 0.7 %copy-start.6 = (f32[4,256]{1,0:T(4,128)S(1)}, f32[4,256]{1,0:T(4,128)}, u32[]{:S(2)}) copy-start(f32[4,256]{1,0:T(4,128)} %skip_gain.1) | copy-start | bytes 12292
  16.3 0.7 %copy-start.7 = (f32[128]{0:T(128)S(1)}, f32[128]{0:T(128)}, u32[]{:S(2)}) copy-start(f32[128]{0:T(128)} %param.16) | copy-start | bytes 1540
  16.3 0.7 %copy-start.8 = (f32[256]{0:T(256)S(1)}, f32[256]{0:T(256)}, u32[]{:S(2)}) copy-start(f32[256]{0:T(256)} %param.19) | copy-start | bytes 3076
  40.3 0.7 %copy-start.13 = (f32[256]{0:T(256)S(1)}, f32[256]{0:T(256)}, u32[]{:S(2)}) copy-start(f32[256]{0:T(256)} %param.26) | copy-start | bytes 3076
